TPU v7x, 32 devices: a whole 2x2x4 slice. The times are simulated.
32 devices in a mesh: dp: 16 (over z, x, core), mp: 2 (over y).
Axes of the slice: x: 2, y: 2, z: 4, core: 2. Of those that a mesh axis runs over, the one named last changes fastest.
Arguments:
- tokens: bfloat16 [8192, 1024], P('dp'), may hold values from -6 to 6
- seq_lengths: int32 [64], P('dp'), may hold values from 0 to 512, as said below
- ln_gain: float32 [4, 1024], replicated, may hold values from 0.1 to 1.9
- ln_bias: float32 [4, 1024], replicated, may hold values from -3 to 3
- w_qkv: bfloat16 [3, 1024, 1024], P(None, 'dp', 'mp'), may hold values from -0.25 to 0.25
- w_out: bfloat16 [1024, 1024], P('mp', 'dp'), may hold values from -0.5 to 0.5
- w_up: bfloat16 [1024, 4096], P('dp', 'mp'), may hold values from -0.1875 to 0.1875
- w_down: bfloat16 [4096, 1024], P('mp', 'dp'), may hold values from -0.09375 to 0.09375
- cotangent: bfloat16 [8192, 1024], P(('dp', 'mp')), may hold values from -6 to 6
Outputs:
- output: bfloat16 [8192, 1024], P(('dp', 'mp'))
- grad_tokens: float32 [8192, 1024], P(('dp', 'mp'))
- grad_qkv: float32 [3, 1024, 1024], P(None, 'dp', 'mp')
- grad_out: float32 [1024, 1024], P('mp', 'dp')
- grad_up: float32 [1024, 4096], P('dp', 'mp')
- grad_down: float32 [4096, 1024], P('mp', 'dp')
- grad_gain: float32 [4, 1024], P(None, 'dp')
- grad_bias: float32 [4, 1024], P(None, 'dp')
Inputs may be any that keep to these rules, and one draw needn't show every extreme that they name: `seq_lengths`: within every group of 512 tokens (blocks of 128), the first block starts a sequence; a sequence that starts at block b and covers n blocks has a length from n * 128 - 128 // 2 + 1 to n * 128, the rest of its last block being padding. In every draw some group holds a single sequence of exactly 512 tokens.
All inputs are finite; a program needn't handle non-finite values.
Results may differ from a plain program's by a relative error of at most 0.023.
Values may be sent and summed in bfloat16 or wider, within the bound.
No kernel may reach another device: no remote copies, remote signals or barrier semaphores. Data moves between devices by JAX's collectives and lax.ppermute only.
A program may use at most 128 MiB of HBM per device.

v0:
```python
import functools

import jax
import jax.numpy as jnp
from jax import lax
from jax.experimental import pallas as pl
from jax.experimental.pallas import tpu as pltpu
from jax.sharding import PartitionSpec as P

HD = 64
BLOCK = 128
LANES = 128
NORM_EPS = 1e-05
ROPE_BASE = 10000.0
MASK_FILL = -1e30
F32 = jnp.float32
BF16 = jnp.bfloat16
VMEM_LIMIT = 6 * 1024 * 1024
STEP = 128
NN = (((1,), (0,)), ((), ()))
NT = (((1,), (1,)), ((), ()))
TN = (((0,), (0,)), ((), ()))


def mm(left, right, dims):
    return lax.dot_general(left, right, dims, preferred_element_type=F32)


def sds(shape, dtype):
    return jax.ShapeDtypeStruct(shape, dtype)


def whole():
    return pl.BlockSpec(memory_space=pltpu.VMEM)


def smem():
    return pl.BlockSpec(memory_space=pltpu.SMEM)


def anywhere():
    return pl.BlockSpec(memory_space=pl.ANY)


TIMES = {
    "prepare": 3.3, "cotangent_rows": 1.5, "qkv_project": 2.0, "attend0": 2.5, "attend1": 4.4,
    "up_project": 4.3, "down_project": 1.3, "mlp_back": 5.4, "mid_norm": 2.5, "last_norm": 3.0, "weight_grad": 1.3, "mid_back": 3.3,
    "attend_back": 5.0, "in_back": 3.6, "gain_pack": 0.4, "tokens_back": 3.9, "stage": 0.5,
    "assemble": 1.2, "ring_sum": 1.3, "ring_end": 2.0, "rotary": 2.0, "split": 0.4,
}
TIME_SHARE = 1.0


def cost_of(name):
    return pl.CostEstimate(
        flops=0, bytes_accessed=int(TIMES[name] * TIME_SHARE * 3.69e6), transcendentals=0
    )


ORDER = {
    "s12": ("stages",), "s13": ("a1",), "s14": ("cot_got",), "s21": ("s14_sent",), "s31": ("s14",),
    "cot_swap": ("s11",), "w1": ("s21",), "rotary": ("own1",), "cot": ("own1",), "s22": ("own1",),
    "qkv": ("cot",), "attend1": ("part0", "s31"), "s23": ("part1",), "s24": ("y0",),
    "norm0": ("own2",), "s34": ("own2", "y1"), "up1": ("down0",), "down1": ("down0",),
    "back1": ("back0",), "up_other": ("down_other",), "down_mine": ("up_other",),
    "up_mine": ("down_mine", "down_far"), "up_near": ("da0", "up_mine"), "mid0": ("m1_sent",),
    "last": ("mid0",), "m2": ("last",), "mid1": ("m2_sent",), "attn_near": ("m2",), "m3": ("attn_other",),
    "in_back": ("m3_sent",), "attn_mine": ("gain_sum",), "gains": ("attn_mine",),
    "part_give": ("gains",), "m4": ("q1_sent",), "q2": ("m4_sent",), "tokens": ("q2_sent",),
    "q3": ("tokens",), "m_end": ("q3_sent",), "q4": ("m_end",),
}


def kernel_call(body, name, out_shape, args, smems=1, flops=0, nbytes=0, scratch=(), **extra):
    many = isinstance(out_shape, (list, tuple))
    return pl.pallas_call(
        body,
        in_specs=[smem()] * smems + [whole()] * (len(args) - smems),
        out_specs=[whole()] * len(out_shape) if many else whole(),
        out_shape=out_shape,
        scratch_shapes=list(scratch),
        compiler_params=pltpu.CompilerParams(vmem_limit_bytes=VMEM_LIMIT),
        cost_estimate=cost_of(name),
        name=name,
        **extra,
    )(*args)


def after(value, *others):
    return lax.optimization_barrier((value,) + others)[0]


def chip_of(place, size):
    if isinstance(place, int):
        return 2 * place if place < size // 2 else 2 * (size - 1 - place) + 1
    return jnp.where(place < size // 2, 2 * place, 2 * (size - 1 - place) + 1)


def ring_order(size):
    order = [size // 2]
    for step in range(size // 2 - 1, 0, -1):
        order += [step, -step]
    return order + [0]


def chip_lanes(ids_ref, width):
    size = width // LANES
    own = ids_ref[0] // 2
    here = jnp.where(own % 2 == 0, own // 2, size - 1 - own // 2)
    starts = [chip_of((here + step + size) % size, size) * LANES for step in ring_order(size)]
    return [pl.ds(pl.multiple_of(start, LANES), LANES) for start in starts]


def split_cores(ids_ref, ref, rows):
    places = chip_lanes(ids_ref, ref.shape[1])
    core = ids_ref[0] % 2
    own, other = [], []
    for i in range(0, len(places), 2):
        a, b = (ref[rows, place].astype(F32) for place in places[i : i + 2])
        low = lax.broadcasted_iota(jnp.int32, a.shape, 1) < LANES // 2
        first = jnp.where(low, a, pltpu.roll(b, LANES // 2, 1))
        second = jnp.where(low, pltpu.roll(a, LANES // 2, 1), b)
        own.append(jnp.where(core == 0, first, second))
        other.append(jnp.where(core == 0, second, first))
    return jnp.concatenate(own + other, axis=1)


def join_cores(ids_ref, values, out_ref, rows):
    places = chip_lanes(ids_ref, values.shape[1])
    core = ids_ref[0] % 2
    half = values.shape[1] // 2
    for i in range(0, len(places), 2):
        own = values[:, i * LANES // 2 : i * LANES // 2 + LANES]
        other = values[:, half + i * LANES // 2 : half + i * LANES // 2 + LANES]
        low = lax.broadcasted_iota(jnp.int32, own.shape, 1) < LANES // 2
        first = jnp.where(core == 0, own, other)
        second = jnp.where(core == 0, other, own)
        joined = (
            jnp.where(low, first, pltpu.roll(second, LANES // 2, 1)),
            jnp.where(low, pltpu.roll(first, LANES // 2, 1), second),
        )
        for place, part in zip(places[i : i + 2], joined):
            out_ref[rows, place] = part.astype(out_ref.dtype)


def norm_stats(values):
    centred = values - jnp.mean(values, axis=-1, keepdims=True)
    rstd = lax.rsqrt(jnp.mean(centred * centred, axis=-1, keepdims=True) + NORM_EPS)
    return centred * rstd, rstd


def norm_back(normed, rstd, scaled_grad):
    first = jnp.mean(scaled_grad, axis=-1, keepdims=True)
    second = jnp.mean(scaled_grad * normed, axis=-1, keepdims=True)
    return (scaled_grad - first - normed * second) * rstd


def fold_rows(values):
    return jnp.sum(values.reshape(-1, 8, values.shape[-1]), axis=0)


def lanes_at(start, count):
    if isinstance(start, int):
        return slice(start, start + count)
    return pl.ds(pl.multiple_of(start, LANES), count)


def from_features(left, w_refs, cols):
    total, start = None, 0
    for ref in w_refs:
        term = mm(left[:, start : start + ref.shape[0]], ref[:, cols], NN)
        total = term if total is None else total + term
        start += ref.shape[0]
    return total


def into_features(out_ref, rows, left, w_refs, cols):
    start = 0
    for ref in w_refs:
        part = mm(left, ref[:, cols], NT).astype(BF16)
        out_ref[rows, start : start + ref.shape[0]] = part
        start += ref.shape[0]


def row_steps(rows, body):
    @pl.loop(0, rows // STEP)
    def _(i):
        body(pl.ds(pl.multiple_of(i * STEP, STEP), STEP))


def prepare_kernel(ids_ref, x_ref, gain_ref, bias_ref, xp_ref, a1_ref, gp_ref, bp_ref):
    every = slice(0, gain_ref.shape[0])
    gp_ref[...] = split_cores(ids_ref, gain_ref, every)
    bp_ref[...] = split_cores(ids_ref, bias_ref, every)

    def body(at):
        x = split_cores(ids_ref, x_ref, at)
        xp_ref[at, :] = x.astype(BF16)
        normed, _ = norm_stats(x)
        a1_ref[at, :] = (normed * gp_ref[0:1, :] + bp_ref[0:1, :]).astype(BF16)

    row_steps(x_ref.shape[0], body)


def prepare(ids, x, gain, bias):
    return kernel_call(
        prepare_kernel,
        "prepare",
        [sds(x.shape, BF16), sds(x.shape, BF16), sds(gain.shape, F32), sds(bias.shape, F32)],
        (ids, x, gain, bias),
        nbytes=6 * x.size,
    )


def cotangent_kernel(ids_ref, own_ref, got_ref, out_ref):
    side = ids_ref[1]
    rows = own_ref.shape[0]
    for ref, base in ((own_ref, side * rows), (got_ref, (1 - side) * rows)):

        @pl.loop(0, rows // STEP)
        def _(i, ref=ref, base=base):
            at = pl.ds(pl.multiple_of(i * STEP, STEP), STEP)
            to = pl.ds(pl.multiple_of(base + i * STEP, STEP), STEP)
            out_ref[to, :] = split_cores(ids_ref, ref, at).astype(BF16)


def cotangent_rows(ids, own, got):
    rows, width = own.shape
    return kernel_call(
        cotangent_kernel, "cotangent_rows", sds((2 * rows, width), BF16), (ids, own, got),
        nbytes=8 * own.size,
    )


def partner(values):
    lane = lax.broadcasted_iota(jnp.int32, values.shape, 1)
    ahead = pltpu.roll(values, LANES - HD // 2, 1)
    behind = pltpu.roll(values, HD // 2, 1)
    return jnp.where(lax.rem(lane, HD) < HD // 2, ahead, behind)


def qkv_kernel(a_ref, cos_ref, sin_ref, *refs):
    w_refs, out_ref = refs[:-1], refs[-1]
    cols = w_refs[0].shape[1] // 4
    rows = 2 * BLOCK

    @pl.loop(0, a_ref.shape[0] // rows)
    def _(i):
        at = pl.ds(pl.multiple_of(i * rows, rows), rows)
        cos, sin = cos_ref[at, :], sin_ref[at, :]
        a = a_ref[at, :]
        for which in range(3):
            proj = from_features(a, w_refs, slice(which * cols, (which + 1) * cols))
            for start in range(0, cols, LANES):
                part = proj[:, start : start + LANES]
                if which < 2:
                    part = part * cos + partner(part) * sin
                if which == 0:
                    part = part.astype(BF16).astype(F32) * HD ** (-0.5)
                out_ref[at, which * cols + start : which * cols + start + LANES] = part.astype(BF16)


def qkv_project(a1, w, cos, sin):
    out = sds((a1.shape[0], w[0].shape[1] // 4 * 3), BF16)
    return kernel_call(qkv_kernel, "qkv_project", out, (a1, cos, sin, *w), smems=0)


def span_of(len_ref, block):
    start, size = jnp.int32(0), jnp.int32(0)
    for b in range(block + 1):
        here = len_ref[b]
        start = jnp.where(here > 0, b * BLOCK, start)
        size = jnp.where(here > 0, here, size)
    return start, start + size


def rotary_kernel(len_ref, cos_ref, sin_ref):
    lane = lax.broadcasted_iota(jnp.int32, (BLOCK, LANES), 1)
    row = lax.broadcasted_iota(jnp.int32, (BLOCK, LANES), 0)
    index = (lane % (HD // 2)).astype(F32)
    frequency = jnp.exp(index * (-2.0 / HD * 9.210340371976184))
    back = lane % HD >= HD // 2
    blocks = cos_ref.shape[0] // BLOCK

    @pl.loop(0, blocks)
    def _(b):
        start = jnp.int32(0)
        for k in range(blocks):
            start = jnp.where((k <= b) & (len_ref[k] > 0), k * BLOCK, start)
        at = pl.ds(pl.multiple_of(b * BLOCK, BLOCK), BLOCK)
        angle = (row + (b * BLOCK - start)).astype(F32) * frequency
        sin = jnp.sin(angle)
        cos_ref[at, :] = jnp.cos(angle)
        sin_ref[at, :] = jnp.where(back, sin, -sin)


def rotary_pair(lengths, count):
    out = sds((count, LANES), F32)
    return kernel_call(rotary_kernel, "rotary", [out, out], (lengths,))


def head_lanes(rows, first):
    lane = lax.broadcasted_iota(jnp.int32, (rows, LANES), 1)
    return (lane < HD) == first


def attend_kernel(row0, len_ref, q_ref, *refs):
    w_refs, (p_ref, o_ref, part_ref) = refs[:-3], refs[-3:]
    rows, cols = o_ref.shape
    ext = p_ref.shape[2]
    key = lax.broadcasted_iota(jnp.int32, (BLOCK, ext), 1)
    query = lax.broadcasted_iota(jnp.int32, (BLOCK, ext), 0)
    masks = []
    for b in range(rows // BLOCK):
        lo, hi = span_of(len_ref, row0 // BLOCK + b)
        seen = (key >= lo) & (key < hi) & (key <= query + (row0 + b * BLOCK))
        masks.append(jnp.where(seen, 0.0, MASK_FILL))
    mask = jnp.concatenate(masks, axis=0)
    head = 0
    for start in range(0, cols, LANES):
        q = q_ref[row0 : row0 + rows, start : start + LANES]
        k = q_ref[0:ext, cols + start : cols + start + LANES]
        v = q_ref[0:ext, 2 * cols + start : 2 * cols + start + LANES]
        outs = []
        for first in (True, False):
            mine = head_lanes(rows, first)
            s = mm(jnp.where(mine, q, jnp.zeros_like(q)), k, NT) + mask
            e = jnp.exp(s - jnp.max(s, axis=-1, keepdims=True))
            p = (e * (1.0 / jnp.sum(e, axis=-1, keepdims=True))).astype(BF16)
            p_ref[head] = p
            head += 1
            outs.append(mm(p, v, NN))
        o_ref[:, start : start + LANES] = jnp.where(
            head_lanes(rows, True), outs[0], outs[1]
        ).astype(BF16)
    into_features(part_ref, slice(None), o_ref[...], w_refs, slice(3 * cols, 4 * cols))


def attend(row0, rows, lengths, qkv, w):
    ext = row0 + rows
    cols = qkv.shape[1] // 3
    width = sum(piece.shape[0] for piece in w)
    return kernel_call(
        functools.partial(attend_kernel, row0),
        "attend0" if row0 == 0 else "attend1",
        [sds((cols // HD, rows, ext), BF16), sds((rows, cols), BF16), sds((rows, width), BF16)],
        (lengths, qkv, *w),
    )


def hidden_of(x, ya, yb, gain_ref, bias_ref):
    n1, r1 = norm_stats(ya.astype(F32) + yb.astype(F32))
    return x.astype(F32) + n1 * gain_ref[1:2, :] + bias_ref[1:2, :], n1, r1


def chunk_rows(chunk, rows, at):
    return pl.ds(pl.multiple_of(chunk * rows + at.start, STEP), STEP)


UNITS = 512


def mid_norm_kernel(chunk, x_ref, ya_ref, yb_ref, gain_ref, bias_ref, a3_ref):
    rows = a3_ref.shape[0]

    def body(at):
        x = x_ref[chunk_rows(chunk, rows, at), :]
        h, _, _ = hidden_of(x, ya_ref[at, :], yb_ref[at, :], gain_ref, bias_ref)
        n2, _ = norm_stats(h)
        a3_ref[at, :] = (n2 * gain_ref[2:3, :] + bias_ref[2:3, :]).astype(BF16)

    row_steps(rows, body)


def mid_norm(chunk, x, ya, yb, gain, bias):
    body = functools.partial(mid_norm_kernel, chunk)
    return kernel_call(body, "mid_norm", sds(ya.shape, BF16), (x, ya, yb, gain, bias), smems=0)


def up_kernel(a3_ref, *refs):
    w_refs, (g_ref, gp_ref) = refs[:-2], refs[-2:]

    @pl.loop(0, w_refs[0].shape[1] // UNITS)
    def _(i):
        to = pl.ds(pl.multiple_of(i * UNITS, UNITS), UNITS)
        u = from_features(a3_ref[...], w_refs, to)
        k0 = 0.7978845608028654
        k1 = 0.044715
        sq = u * u
        th = jnp.tanh(u * (k0 + (k0 * k1) * sq))
        plus = 0.5 + 0.5 * th
        g_ref[:, to] = (u * plus).astype(BF16)
        slope = plus + (u * (k0 + (3.0 * k0 * k1) * sq)) * (0.5 - (0.5 * th) * th)
        gp_ref[:, to] = slope.astype(BF16)


def up_project(a3, w):
    out = sds((a3.shape[0], w[0].shape[1]), BF16)
    return kernel_call(up_kernel, "up_project", [out, out], (a3, *w), smems=0)


def down_kernel(g_ref, *refs):
    into_features(refs[-1], slice(None), g_ref[...], refs[:-1], slice(None))


def down_project(g, w):
    out = sds((g.shape[0], sum(piece.shape[0] for piece in w)), BF16)
    return kernel_call(down_kernel, "down_project", out, (g, *w), smems=0)


def mlp_back_kernel(chunk, za_ref, zb_ref, cot_ref, gain_ref, gp_ref, *refs):
    dz_ref, du_ref, part_ref = refs[-3:]
    pieces = (len(refs) - 3) // 2
    w3, w2 = refs[:pieces], refs[pieces : 2 * pieces]
    rows = za_ref.shape[0]

    def body(at):
        n3, r3 = norm_stats(za_ref[at, :].astype(F32) + zb_ref[at, :].astype(F32))
        cot = cot_ref[chunk_rows(chunk, rows, at), :].astype(F32)
        dz_ref[at, :] = norm_back(n3, r3, cot * gain_ref[3:4, :]).astype(BF16)

    row_steps(rows, body)

    @pl.loop(0, w3[0].shape[1] // UNITS)
    def _(i):
        to = pl.ds(pl.multiple_of(i * UNITS, UNITS), UNITS)
        dg = from_features(dz_ref[...], w3, to)
        du_ref[:, to] = (dg * gp_ref[:, to].astype(F32)).astype(BF16)

    into_features(part_ref, slice(None), du_ref[...], w2, slice(None))


def mlp_back(chunk, za, zb, cot, gain, gp, w3, w2):
    rows, width = za.shape
    units = gp.shape[1]
    return kernel_call(
        functools.partial(mlp_back_kernel, chunk),
        "mlp_back",
        [sds((rows, width), BF16), sds((rows, units), BF16), sds((rows, width), BF16)],
        (za, zb, cot, gain, gp, *w3, *w2),
        smems=0,
    )


def last_norm_kernel(ids_ref, x_ref, cot_ref, gain_ref, bias_ref, *refs):
    ys, zs, (out_ref, gb_ref) = refs[0:4], refs[4:8], refs[8:]
    rows = out_ref.shape[0]
    gb_ref[...] = jnp.zeros_like(gb_ref)
    for chunk in range(2):
        ya_ref, yb_ref = ys[2 * chunk : 2 * chunk + 2]
        za_ref, zb_ref = zs[2 * chunk : 2 * chunk + 2]

        def body(at, chunk=chunk, ya_ref=ya_ref, yb_ref=yb_ref, za_ref=za_ref, zb_ref=zb_ref):
            far = chunk_rows(chunk, rows, at)
            n3, _ = norm_stats(za_ref[at, :].astype(F32) + zb_ref[at, :].astype(F32))
            cot = cot_ref[far, :].astype(F32)
            gb_ref[0] += fold_rows(cot * n3)
            gb_ref[1] += fold_rows(cot)

            @pl.when(ids_ref[1] == chunk)
            def _():
                h, _, _ = hidden_of(x_ref[far, :], ya_ref[at, :], yb_ref[at, :], gain_ref, bias_ref)
                out = h + (n3 * gain_ref[3:4, :] + bias_ref[3:4, :])
                join_cores(ids_ref, out, out_ref, at)

        row_steps(rows, body)


def last_norm(ids, x, cot, gain, bias, ys, zs):
    rows, width = ys[0][0].shape
    return kernel_call(
        last_norm_kernel,
        "last_norm",
        [sds((rows, width), BF16), sds((2, 8, width), F32)],
        (ids, x, cot, gain, bias, *ys[0], *ys[1], *zs[0], *zs[1]),
    )


def weight_grad_kernel(which, sizes, *refs):
    far_ref, near_ref, left_sc = refs[-3:]
    half, block = left_sc.shape[0], far_ref.shape[0]
    start = 0
    for lefts, rights, cols in sizes:
        rows = 0
        for ref in refs[lefts[0] : lefts[1]]:
            part = ref[:, which * half : (which + 1) * half]
            left_sc[:, rows : rows + part.shape[0]] = part.T
            rows += part.shape[0]

        def blocks(first, count, rights=rights, start=start):
            for i in range(count):
                c = (first + i) * UNITS
                total, rows = None, 0
                for ref in refs[rights[0] : rights[1]]:
                    n = ref.shape[0]
                    term = mm(left_sc[:, rows : rows + n], ref[:, lanes_at(c, UNITS)], NN)
                    total = term if total is None else total + term
                    rows += n
                total = total.astype(BF16)
                far_ref[:, lanes_at(start + c, UNITS)] = total[:block]
                near_ref[:, lanes_at(start + c, UNITS)] = total[block:]

        pairs = cols // (2 * UNITS)
        if pairs > 1:
            pl.loop(0, pairs)(lambda i: blocks(2 * i, 2))
        else:
            blocks(0, cols // UNITS)
        start += cols


def weight_grad(which, size, products):
    args, sizes, total = [], [], 0
    for lefts, rights in products:
        cols = rights[0].shape[1]
        n = len(args)
        sizes.append(((n, n + len(lefts)), (n + len(lefts), n + len(lefts) + len(rights)), cols))
        args += list(lefts) + list(rights)
        total += cols
    half = args[0].shape[1] // 2
    count = sum(a.shape[0] for a in products[0][0])
    block = half // size
    return kernel_call(
        functools.partial(weight_grad_kernel, which, sizes),
        "weight_grad",
        [sds((block, total), BF16), sds((half - block, total), BF16)],
        tuple(args),
        smems=0,
        scratch=[pltpu.VMEM((half, count), BF16)],
    )


def mid_back_kernel(
    chunk, x_ref, ya_ref, yb_ref, ea_ref, eb_ref, cot_ref, gain_ref, bias_ref, *refs
):
    w_refs, (dh_ref, dy_ref, do_ref, gb_ref) = refs[:-4], refs[-4:]
    rows, cols = do_ref.shape
    gb_ref[...] = jnp.zeros_like(gb_ref)

    def body(at):
        far = chunk_rows(chunk, rows, at)
        h, n1, r1 = hidden_of(x_ref[far, :], ya_ref[at, :], yb_ref[at, :], gain_ref, bias_ref)
        n2, r2 = norm_stats(h)
        e = ea_ref[at, :].astype(F32) + eb_ref[at, :].astype(F32)
        dh = cot_ref[far, :].astype(F32) + norm_back(n2, r2, e * gain_ref[2:3, :])
        dh_ref[at, :] = dh
        dy_ref[at, :] = norm_back(n1, r1, dh * gain_ref[1:2, :]).astype(BF16)
        gb_ref[0] += fold_rows(e * n2)
        gb_ref[1] += fold_rows(e)
        gb_ref[2] += fold_rows(dh * n1)
        gb_ref[3] += fold_rows(dh)

    row_steps(rows, body)
    do = from_features(dy_ref[...], w_refs, slice(3 * cols, 4 * cols))
    do_ref[...] = do.astype(BF16)


def mid_back(chunk, x, ya, yb, ea, eb, cot, gain, bias, w):
    rows, width = ea.shape
    cols = w[0].shape[1] // 4
    return kernel_call(
        functools.partial(mid_back_kernel, chunk),
        "mid_back",
        [
            sds((rows, width), F32),
            sds((rows, width), BF16),
            sds((rows, cols), BF16),
            sds((4, 8, width), F32),
        ],
        (x, ya, yb, ea, eb, cot, gain, bias, *w),
        smems=0,
        flops=2 * rows * width * cols,
    )


def attend_back_kernel(q_ref, p0_ref, p1_ref, o0, o1, d0, d1, cos_ref, sin_ref, g_ref):
    rows, cols = o0.shape

    @pl.loop(0, cols // LANES)
    def _(i):
        cos, sin = cos_ref[...], sin_ref[...]
        start = i * LANES
        at = lanes_at(start, LANES)
        q = q_ref[:, at]
        k = q_ref[:, lanes_at(cols + start, LANES)]
        v = q_ref[:, lanes_at(2 * cols + start, LANES)]
        do = (d0[:, at], d1[:, at])
        prod = [a.astype(F32) * b[:, at].astype(F32) for a, b in zip(do, (o0, o1))]
        dq, dk, dv = [], [], []
        for turn, first in enumerate((True, False)):
            mine = head_lanes(rows, first)
            dqs = []
            for c, p_ref in enumerate((p0_ref, p1_ref)):
                ext = p_ref.shape[2]
                p = p_ref[2 * i + turn]
                dp = mm(jnp.where(mine, do[c], jnp.zeros_like(do[c])), v[:ext], NT)
                dot = jnp.sum(jnp.where(mine, prod[c], 0.0), axis=-1, keepdims=True)
                ds = (p.astype(F32) * (dp - dot)).astype(BF16)
                dqs.append(mm(ds, k[:ext], NN))
                dkc = mm(ds, q[c * rows : (c + 1) * rows], TN)
                dvc = mm(p, do[c], TN)
                if c == 0:
                    dk0, dv0 = dkc, dvc
            dk.append(jnp.concatenate([dk0 + dkc[:rows], dkc[rows:]], axis=0))
            dv.append(jnp.concatenate([dv0 + dvc[:rows], dvc[rows:]], axis=0))
            dq.append(jnp.concatenate(dqs, axis=0))
        low = head_lanes(2 * rows, True)
        gq = jnp.where(low, dq[0], dq[1]) * HD ** (-0.5)
        gk = jnp.where(low, dk[0], dk[1])
        gv = jnp.where(low, dv[0], dv[1])
        g_ref[:, at] = (gq * cos - partner(gq) * sin).astype(BF16)
        g_ref[:, lanes_at(cols + start, LANES)] = (gk * cos - partner(gk) * sin).astype(BF16)
        g_ref[:, lanes_at(2 * cols + start, LANES)] = gv.astype(BF16)


def attend_back(qkv, probs, outs, grads, cos, sin):
    count, three = qkv.shape
    heads = probs[0].shape[0]
    return kernel_call(
        attend_back_kernel,
        "attend_back",
        sds((count, three), BF16),
        (qkv, *probs, *outs, *grads, cos, sin),
        smems=0,
        flops=10 * heads * count * count * HD,
    )


def in_back_kernel(ids_ref, g_ref, x_ref, *refs):
    w_refs, (keep_ref, give_ref, gb_ref) = refs[:-3], refs[-3:]
    three = g_ref.shape[1]
    rows = keep_ref.shape[0]
    gb_ref[...] = jnp.zeros_like(gb_ref)
    for turn, out_ref in enumerate((give_ref, keep_ref)):
        base = (1 - ids_ref[1] if turn == 0 else ids_ref[1]) * rows
        g = g_ref[pl.ds(pl.multiple_of(base, rows), rows), :]
        into_features(out_ref, slice(None), g, w_refs, slice(0, three))

        @pl.loop(0, rows // STEP)
        def _(i, base=base, out_ref=out_ref):
            e = out_ref[pl.ds(pl.multiple_of(i * STEP, STEP), STEP), :].astype(F32)
            far = pl.ds(pl.multiple_of(base + i * STEP, STEP), STEP)
            n0, _ = norm_stats(x_ref[far, :].astype(F32))
            gb_ref[0] += fold_rows(e * n0)
            gb_ref[1] += fold_rows(e)


def in_back(ids, g, x, w):
    count, three = g.shape
    width = x.shape[1]
    part = sds((count // 2, width), BF16)
    return kernel_call(
        in_back_kernel, "in_back", [part, part, sds((2, 8, width), F32)], (ids, g, x, *w),
    )


def gain_sum_kernel(gb0_ref, g12a, g12b, g3, mine_ref, other_ref):
    share = 0.5
    rows = []
    for kind in range(2):
        rows += [
            gb0_ref[kind],
            share * (g12a[2 + kind] + g12b[2 + kind]),
            share * (g12a[kind] + g12b[kind]),
            share * g3[kind],
        ]
    half = mine_ref.shape[1]
    for i, row in enumerate(rows):
        row = jnp.sum(row, axis=0, keepdims=True)
        mine_ref[i : i + 1, :] = row[:, :half]
        other_ref[i : i + 1, :] = row[:, half:]


def gain_sum(gb0, g12, g3):
    out = sds((8, gb0.shape[-1] // 2), F32)
    return kernel_call(gain_sum_kernel, "gain_pack", [out, out], (gb0, *g12, g3), smems=0)


def gain_pack_kernel(*refs):
    out_ref = refs[-1]
    total = refs[0][...] + refs[1][...] + refs[2][...] + refs[3][...]
    filler = jnp.zeros((LANES - total.shape[0], total.shape[1]), F32)
    out_ref[...] = jnp.concatenate([total, filler], axis=0).T.astype(BF16)


def gain_pack(parts):
    out = sds((parts[0].shape[1], LANES), BF16)
    return kernel_call(gain_pack_kernel, "gain_pack", out, tuple(parts), smems=0)


def tokens_back_kernel(ids_ref, x_ref, keep_ref, got_ref, dh0_ref, dh1_ref, gain_ref, out_ref):
    side = ids_ref[1]
    rows = got_ref.shape[0]

    def body(at):
        far = pl.ds(pl.multiple_of(side * rows + at.start, STEP), STEP)
        e = keep_ref[at, :].astype(F32) + got_ref[at, :].astype(F32)
        n0, r0 = norm_stats(x_ref[far, :].astype(F32))
        dh = jnp.where(side == 0, dh0_ref[at, :], dh1_ref[at, :])
        join_cores(ids_ref, dh + norm_back(n0, r0, e * gain_ref[0:1, :]), out_ref, at)

    row_steps(rows, body)


def tokens_back(ids, x, keep, got, dhs, gain):
    return kernel_call(
        tokens_back_kernel, "tokens_back", sds(got.shape, F32), (ids, x, keep, got, *dhs, gain),
    )


def split_kernel(up_ref, down_ref, up_out, down_out):
    half = up_out.shape[0]
    up_out[...] = up_ref[:half, :]
    down_out[...] = down_ref[half:, :]


def split(up, down):
    out = sds((up.shape[0] // 2, up.shape[1]), BF16)
    return kernel_call(split_kernel, "split", [out, out], (up, down), smems=0)


def stage_kernel(*refs):
    ins, out_ref, sem = refs[:-2], refs[-2], refs[-1]
    copies, start = [], 0
    for ref in ins:
        parts = [ref.at[i] for i in range(ref.shape[0])] if len(ref.shape) == 3 else [ref]
        for part in parts:
            cols = part.shape[1]
            dst = out_ref.at[:, pl.ds(start, cols)]
            copies.append(pltpu.make_async_copy(part, dst, sem.at[len(copies)]))
            start += cols
    for copy in copies:
        copy.start()
    for copy in copies:
        copy.wait()


def stage(*arrays):
    rows = arrays[0].shape[-2]
    cols = sum(a.size // rows for a in arrays)
    return pl.pallas_call(
        stage_kernel,
        in_specs=[pl.BlockSpec(memory_space=pltpu.HBM)] * len(arrays),
        out_specs=whole(),
        out_shape=sds((rows, cols), BF16),
        scratch_shapes=[pltpu.SemaphoreType.DMA((4 * len(arrays),))],
        compiler_params=pltpu.CompilerParams(vmem_limit_bytes=VMEM_LIMIT),
        cost_estimate=cost_of("stage"),
        name="stage",
    )(*arrays)


def assemble_kernel(places, *refs):
    ins, out, sem = refs[: len(places)], refs[-2], refs[-1]
    copies = []
    for i, (src, at) in enumerate(zip(ins, places)):
        copies.append(pltpu.make_async_copy(src, out.at[pl.ds(at, src.shape[0])], sem.at[i]))
    for copy in copies:
        copy.start()
    for copy in copies:
        copy.wait()


def assemble(places, pieces):
    rows = sum(piece.shape[0] for piece in pieces)
    return pl.pallas_call(
        functools.partial(assemble_kernel, places),
        in_specs=[anywhere()] * len(pieces),
        out_specs=whole(),
        out_shape=sds((rows, pieces[0].shape[1]), BF16),
        scratch_shapes=[pltpu.SemaphoreType.DMA((len(pieces),))],
        compiler_params=pltpu.CompilerParams(vmem_limit_bytes=VMEM_LIMIT),
        cost_estimate=cost_of("assemble"),
        name="assemble",
    )(*pieces)


def term_rows(groups, block, index, to):
    total = None
    for refs in groups:
        if len(refs) == 2:
            ref, first = (refs[0], 0) if index == 0 else (refs[1], (index - 1) * block)
        else:
            ref, first = refs[0], index * block
        part = ref[first : first + block, to].astype(F32)
        total = part if total is None else total + part
    return total


def unflatten(refs, layout):
    groups, n = [], 0
    for terms in layout:
        group = []
        for count in terms:
            group.append(refs[n : n + count])
            n += count
        groups.append(group)
    return groups, refs[n:]


def ring_sum_kernel(layout, block, index, way, *refs):
    groups, refs = unflatten(refs, layout)
    out_ref, came = refs[-1], refs[:-1]
    half = block // 2
    start = 0
    for group in groups:
        cols = group[0][0].shape[1]
        for c in range(0, cols, UNITS):
            n = min(UNITS, cols - c)
            own, to = slice(c, c + n), slice(start + c, start + c + n)
            if index == 0:
                rows = slice(way * half, (way + 1) * half)
                total = sum(term[0][rows, own].astype(F32) for term in group)
                out_ref[:, to] = total.astype(BF16)
                continue
            total = term_rows(group, block, index + way, own)
            part = came[0][:, to].astype(F32)
            if part.shape[0] == block:
                out_ref[:, to] = (total + part).astype(BF16)
            else:
                hit = slice(0, half) if way == 0 else slice(half, block)
                rest = slice(half, block) if way == 0 else slice(0, half)
                out_ref[hit, to] = (total[hit] + part).astype(BF16)
                out_ref[rest, to] = total[rest].astype(BF16)
        start += cols


def ring_sum(index, way, block, groups, came=()):
    layout = [[len(term) for term in group] for group in groups]
    flat = [a for group in groups for term in group for a in term]
    cols = sum(group[0][0].shape[1] for group in groups)
    return kernel_call(
        functools.partial(ring_sum_kernel, layout, block, index, way), "ring_sum",
        sds((block // 2 if index == 0 else block, cols), BF16), (*flat, *came), smems=0,
    )


def ring_end_kernel(layout, splits, index, *refs):
    groups, refs = unflatten(refs, layout)
    (up, down), outs = refs[:2], refs[2:]
    block = up.shape[0]
    start, o = 0, 0
    for group, sizes in zip(groups, splits):
        here = 0
        for count, cols in sizes:
            for i in range(max(count, 1)):
                to, own = slice(start, start + cols), slice(here, here + cols)
                total = term_rows(group, block, index, own)
                total = total + up[:, to].astype(F32) + down[:, to].astype(F32)
                if count == 0:
                    turned = total.T
                    outs[o][...] = turned[0:4, :]
                    outs[o + 1][...] = turned[4:8, :]
                elif count > 1:
                    outs[o][i] = total
                else:
                    outs[o][...] = total
                start, here = start + cols, here + cols
            o += 2 if count == 0 else 1


def ring_end(size, groups, came, splits):
    layout = [[len(term) for term in group] for group in groups]
    flat = [a for group in groups for term in group for a in term]
    block = came[0].shape[0]
    shapes = []
    for sizes in splits:
        for count, cols in sizes:
            if count == 0:
                shapes += [(4, block)] * 2
            else:
                shapes.append((count, block, cols) if count > 1 else (block, cols))
    return kernel_call(
        functools.partial(ring_end_kernel, layout, splits, size - 1), "ring_end",
        [sds(shape, F32) for shape in shapes], (*flat, *came), smems=0,
    )


class Ring:
    def __init__(self, n_dp, ids):
        self.size = n_dp // 2
        self.ids = ids
        self.up = self.shift(1)
        self.down = self.shift(-1)
        self.cores = [(i, i ^ 1) for i in range(n_dp)]

    def shift(self, by):
        return [
            (2 * chip_of(p, self.size) + c, 2 * chip_of((p + by) % self.size, self.size) + c)
            for p in range(self.size)
            for c in range(2)
        ]


def swap_cores(ring, value):
    return lax.ppermute(value, "dp", ring.cores)


class Gather:
    def __init__(self, ring, piece):
        self.ring = ring
        self.rows = piece.shape[0]
        self.pieces, self.places = [piece], [ring_order(ring.size).index(0) * self.rows]
        self.step_now = 0
        self.up = self.down = piece

    def step(self, *deps):
        self.step_now += 1
        ring, step = self.ring, self.step_now
        up, down = self.up, self.down
        if deps:
            up, down = after(up, *deps), after(down, *deps)
        shift = 0
        if step == ring.size // 2:
            shift = up.shape[0] // 2
            up, down = split(up, down)
            self.sent = up, down
        self.up = lax.ppermute(up, "dp", ring.up)
        self.down = lax.ppermute(down, "dp", ring.down)
        self.pieces += [self.up, self.down]
        order = ring_order(ring.size)
        self.places += [
            order.index(step if shift else -step) * self.rows,
            order.index(step) * self.rows + shift,
        ]
        return self.up, self.down

    def end(self, *deps):
        pieces = self.pieces
        if deps:
            pieces = [after(pieces[0], *deps), *pieces[1:]]
        return assemble(self.places, pieces)


class Reduce:
    def __init__(self, ring, block, groups):
        self.ring, self.block, self.groups = ring, block, groups
        self.index = 0
        self.came = ()

    def step(self, *deps):
        groups = self.groups
        if deps:
            first = groups[0][0]
            groups = [[(after(first[0], *deps), *first[1:]), *groups[0][1:]], *groups[1:]]
        if self.index == 0:
            groups = [[(term[0],) for term in group] for group in groups]
        sent, came = [], []
        for way, perm in enumerate((self.ring.up, self.ring.down)):
            sent.append(ring_sum(self.index, way, self.block, groups, self.came[way : way + 1]))
            came.append(lax.ppermute(sent[way], "dp", perm))
        self.sent, self.came = tuple(sent), tuple(came)
        self.index += 2 if self.index else 1
        return self.came

    def end(self, splits, *deps):
        came = self.came
        if deps:
            came = after(came[0], *deps), came[1]
        return ring_end(self.ring.size, self.groups, came, splits)


def per_device(n_dp, tokens, seq_lengths, ln_gain, ln_bias, w_qkv, w_out, w_up, w_down, cotangent):
    ids = jnp.stack([lax.axis_index("dp"), lax.axis_index("mp")]).astype(jnp.int32)
    ring = Ring(n_dp, ids)
    count, width = tokens.shape
    rows = count // 2
    w_rows, units = w_up.shape
    cols = w_out.shape[0]

    def swap_sides(value):
        return lax.ppermute(value, "mp", [(0, 1), (1, 0)])

    done = {}

    def dep(name):
        found = []
        for other in ORDER.get(name, ()):
            value = done[other]
            found += list(value) if isinstance(value, (tuple, list)) else [value]
        return found

    def tie(value, name):
        others = dep(name)
        return after(value, *others) if others else value

    def both(own, name):
        return [own, swap_cores(ring, tie(own, name))]

    g1 = Gather(ring, stage(after(w_qkv, ids), w_out.T))
    done["s11"] = g1.step()
    cot_got = done["cot_got"] = swap_sides(tie(cotangent, "cot_swap"))
    stage2, stage3 = stage(w_up), stage(w_down.T)
    done["stages"] = stage2, stage3
    done["s12"] = g1.step(*dep("s12"))
    x, a1, gain, bias = prepare(ids, tokens, ln_gain, ln_bias)
    done["a1"] = a1
    done["s13"] = g1.step(*dep("s13"))
    done["s14"] = g1.step(*dep("s14"))
    done["s14_sent"] = g1.sent
    g2 = Gather(ring, tie(stage2, "s21"))
    done["s21"] = g2.step()
    g3 = Gather(ring, tie(stage3, "s31"))
    done["s31"] = g3.step()
    own = done["own1"] = g1.end(*dep("own1"))
    w1 = both(own, "w1")
    cos, sin = rotary_pair(tie(seq_lengths, "rotary"), count)
    cot = done["cot"] = cotangent_rows(tie(ids, "cot"), cotangent, cot_got)
    done["s22"] = g2.step(*dep("s22"))
    qkv = done["qkv"] = qkv_project(tie(a1, "qkv"), w1, cos, sin)
    probs, outs, ys, a3s, mids, zs, backs, mid_backs = [], [], [], [], [], [], [], []
    for c in range(2):
        p, o, part = attend(c * rows, rows, tie(seq_lengths, f"attend{c}"), qkv, w1)
        probs.append(p)
        outs.append(o)
        done[f"part{c}"] = part
        if c == 0:
            ys.append((part, swap_sides(part)))
            done["y0"] = ys[0][1]
    done["s32"] = g3.step(*dep("s32"))
    done["s23"] = g2.step(*dep("s23"))
    ys.append((part, swap_sides(tie(part, "y1"))))
    done["y1"] = ys[1][1]
    done["s33"] = g3.step(*dep("s33"))
    done["s24"] = g2.step(*dep("s24"))
    own = done["own2"] = g2.end(*dep("own2"))
    w2 = both(own, "w2")
    a3s.append(mid_norm(0, tie(x, "norm0"), *ys[0], gain, bias))
    done["norm0"] = a3s[0]
    done["s34"] = g3.step(*dep("s34"))
    own = done["own3"] = g3.end(*dep("own3"))
    w3 = both(own, "w3")
    mids.append(up_project(tie(a3s[0], "up0"), w2))
    done["up0"] = mids[0][0]
    part = down_project(tie(mids[0][0], "down0"), w3)
    done["down0"] = part
    zs.append((part, swap_sides(part)))
    a3s.append(mid_norm(1, tie(x, "norm1"), *ys[1], gain, bias))
    done["norm1"] = a3s[1]
    mids.append(up_project(tie(a3s[1], "up1"), w2))
    done["up1"] = mids[1][0]
    part = down_project(tie(mids[1][0], "down1"), w3)
    done["down1"] = part
    zs.append((part, swap_sides(part)))
    for c in range(2):
        z = zs[c][0], tie(zs[c][1], f"back{c}")
        dz, du, part = mlp_back(c, *z, cot, gain, mids[c][1], w3, w2)
        backs.append((dz, du, (part, swap_sides(part))))
        done[f"back{c}"], done[f"da{c}"] = dz, backs[c][2][1]
    dzs, dus = [b[0] for b in backs], [b[1] for b in backs]
    gs = [m[0] for m in mids]

    def mid(c):
        w = mid_back(c, tie(x, f"mid{c}"), *ys[c], *backs[c][2], cot, gain, bias, w1)
        done[f"mid{c}"] = w[0]
        mid_backs.append(w)

    def grad(which, products, name):
        others = dep(name)
        if others:
            (lefts, rights), rest = products[0], products[1:]
            products = [([after(lefts[0], *others), *lefts[1:]], rights), *rest]
        term = weight_grad(which, ring.size, products)
        done[name] = term[0]
        return term

    def swap_term(term, name):
        far = swap_cores(ring, term[0])
        done[name + "_far"] = far
        return far, swap_cores(ring, after(term[1], far, *dep(name + "_near")))

    def ring_step(reduce, name):
        done[name] = reduce.step(*dep(name))
        done[name + "_sent"] = reduce.sent

    down_other = grad(1, [(dzs, gs)], "down_other")
    up_other = grad(1, [(a3s, dus)], "up_other")
    down_mine = grad(0, [(dzs, gs)], "down_mine")
    down_got = swap_term(down_other, "down")
    up_mine = grad(0, [(a3s, dus)], "up_mine")
    up_got = swap_term(up_other, "up")
    mlp_ring = Reduce(ring, w_rows, [[down_mine, down_got], [up_mine, up_got]])
    ring_step(mlp_ring, "m1")
    mid(0)
    output, gb3 = last_norm(tie(ids, "last"), x, cot, gain, bias, ys, zs)
    done["last"] = output
    ring_step(mlp_ring, "m2")
    mid(1)
    grads = [m[2] for m in mid_backs]
    g_qkv = done["g_qkv"] = attend_back(tie(qkv, "g_qkv"), probs, outs, grads, cos, sin)
    attn_products = [([a1], [g_qkv]), ([m[1] for m in mid_backs], outs)]
    attn_other = grad(1, attn_products, "attn_other")
    attn_got = swap_term(attn_other, "attn")
    ring_step(mlp_ring, "m3")
    part_keep, part_give, gb0 = in_back(ids, tie(g_qkv, "in_back"), x, w1)
    done["in_back"] = part_keep
    gain_mine, gain_other = gain_sum(gb0, [m[3] for m in mid_backs], gb3)
    done["gain_sum"] = gain_mine
    gain_terms = [
        gain_mine,
        swap_cores(ring, gain_other),
        swap_sides(gain_mine),
        lax.ppermute(gain_other, ("dp", "mp"), [(i, i ^ 3) for i in range(2 * n_dp)]),
    ]
    attn_mine = grad(0, attn_products, "attn_mine")
    gains = gain_pack([tie(gain_terms[0], "gains"), *gain_terms[1:]])
    done["gains"] = gains
    part_got = done["part_got"] = swap_sides(tie(part_give, "part_give"))
    attn_ring = Reduce(ring, w_rows, [[attn_mine, attn_got], [(gains,)]])
    ring_step(attn_ring, "q1")
    ring_step(mlp_ring, "m4")
    ring_step(attn_ring, "q2")
    grad_tokens = done["tokens"] = tokens_back(
        tie(ids, "tokens"), x, part_keep, part_got, [m[0] for m in mid_backs], gain
    )
    ring_step(attn_ring, "q3")
    grad_down, grad_up = mlp_ring.end([[(1, units)], [(1, units)]], *dep("m_end"))
    done["m_end"] = grad_down
    ring_step(attn_ring, "q4")
    grad_qkv, grad_out, grad_gain, grad_bias = attn_ring.end([[(3, cols), (1, cols)], [(0, LANES)]])
    return output, grad_tokens, grad_qkv, grad_out.T, grad_up, grad_down.T, grad_gain, grad_bias


def layer_norm(values, norm_gain, norm_bias):
    average = jnp.mean(values, axis=-1, keepdims=True)
    centred = values - average
    variance = jnp.mean(centred * centred, axis=-1, keepdims=True)
    return centred * lax.rsqrt(variance + NORM_EPS) * norm_gain + norm_bias


def norm_pull(values, norm_gain, norm_bias, grad_result):
    result, puller = jax.vjp(layer_norm, values, norm_gain, norm_bias)
    return puller(grad_result)


def seq_layout(lengths, block_size):
    block_count = lengths.shape[0]
    block_ids = jnp.arange(block_count, dtype=jnp.int32)
    starts = lengths > 0
    earlier = starts[None, :] & (block_ids[None, :] <= block_ids[:, None])
    owners = jnp.max(jnp.where(earlier, block_ids[None, :], 0), axis=1)
    owner_len = jnp.sum(
        jnp.where(block_ids[None, :] == owners[:, None], lengths[None, :], 0), axis=1
    )
    places = jnp.arange(block_count * block_size, dtype=jnp.int32)
    tok_owner = jnp.repeat(owners, block_size)
    position = places - tok_owner * block_size
    is_valid = position < jnp.repeat(owner_len, block_size)
    allowed = (
        (tok_owner[:, None] == tok_owner[None, :])
        & (places[None, :] <= places[:, None])
        & is_valid[None, :]
    )
    return (position, allowed)


def rotary_tables(position, width):
    frequency = ROPE_BASE ** (-jnp.arange(width // 2, dtype=jnp.float32) * 2.0 / width)
    angles = position.astype(jnp.float32)[:, None] * frequency[None, :]
    return (jnp.cos(angles), jnp.sin(angles))


def rotate(values, cos_table, sin_table):
    half_width = values.shape[-1] // 2
    front_half = values[..., :half_width]
    back_half = values[..., half_width:]
    cos_part = cos_table[:, None, :]
    sin_part = sin_table[:, None, :]
    return jnp.concatenate(
        [
            front_half * cos_part - back_half * sin_part,
            back_half * cos_part + front_half * sin_part,
        ],
        axis=-1,
    )


def attention_scores(queries, keys_rot, allowed, scale):
    raw_scores = (
        jnp.einsum("hqd,hkd->hqk", queries, keys_rot, preferred_element_type=jnp.float32) * scale
    )
    return jnp.where(allowed[None, :, :], raw_scores, MASK_FILL)


def plain_device(tokens, seq_lengths, ln_gain, ln_bias, w_qkv, w_out, w_up, w_down, cotangent):
    full_qkv, full_out, full_up, full_down = (
        lax.all_gather(w_qkv, "dp", axis=1, tiled=True),
        lax.all_gather(w_out, "dp", axis=1, tiled=True),
        lax.all_gather(w_up, "dp", axis=0, tiled=True),
        lax.all_gather(w_down, "dp", axis=1, tiled=True),
    )
    tok_count = tokens.shape[0]
    shard_rows = cotangent.shape[0]
    row_start = lax.axis_index("mp") * shard_rows
    heads_here = full_out.shape[0] // HD
    scale = HD ** (-0.5)
    position, allowed = seq_layout(seq_lengths, BLOCK)
    cos_table, sin_table = rotary_tables(position, HD)

    def to_heads(values):
        return jnp.transpose(values.reshape(tok_count, heads_here, HD), (1, 0, 2))

    def from_heads(values):
        return jnp.transpose(values, (1, 0, 2)).reshape(tok_count, heads_here * HD)

    def rotated(values):
        return rotate(values.reshape(tok_count, heads_here, HD), cos_table, sin_table)

    inputs = tokens.astype(jnp.float32)
    normed_in = layer_norm(inputs, ln_gain[0], ln_bias[0]).astype(jnp.bfloat16)
    projected = jnp.einsum("td,cde->cte", normed_in, full_qkv, preferred_element_type=jnp.float32)
    queries = jnp.transpose(rotated(projected[0]), (1, 0, 2)).astype(jnp.bfloat16)
    keys_rot = jnp.transpose(rotated(projected[1]), (1, 0, 2)).astype(jnp.bfloat16)
    values_h = to_heads(projected[2]).astype(jnp.bfloat16)
    scores = attention_scores(queries, keys_rot, allowed, scale)
    top_score = jnp.max(scores, axis=-1, keepdims=True)
    expo = jnp.exp(scores - top_score)
    row_total = jnp.sum(expo, axis=-1, keepdims=True)
    probs = expo / row_total
    log_total = top_score + jnp.log(row_total)
    attended = jnp.einsum(
        "hqk,hkd->hqd", probs.astype(jnp.bfloat16), values_h, preferred_element_type=jnp.float32
    )
    mixed_heads = from_heads(attended).astype(jnp.bfloat16)
    attn_part = jnp.dot(mixed_heads, full_out, preferred_element_type=jnp.float32)
    attn_sum = lax.psum_scatter(
        attn_part.astype(jnp.bfloat16), "mp", scatter_dimension=0, tiled=True
    ).astype(jnp.float32)
    resid_in = lax.dynamic_slice_in_dim(inputs, row_start, shard_rows, 0)
    hidden_state = resid_in + layer_norm(attn_sum, ln_gain[1], ln_bias[1])
    normed_mid = layer_norm(hidden_state, ln_gain[2], ln_bias[2]).astype(jnp.bfloat16)
    mlp_input = lax.all_gather(normed_mid, "mp", axis=0, tiled=True)
    pre_act = jnp.dot(mlp_input, full_up, preferred_element_type=jnp.float32)
    act_low = jax.nn.gelu(pre_act, approximate=True).astype(jnp.bfloat16)
    mlp_part = jnp.dot(act_low, full_down, preferred_element_type=jnp.float32)
    mlp_sum = lax.psum_scatter(
        mlp_part.astype(jnp.bfloat16), "mp", scatter_dimension=0, tiled=True
    ).astype(jnp.float32)
    output = (hidden_state + layer_norm(mlp_sum, ln_gain[3], ln_bias[3])).astype(jnp.bfloat16)
    grad_result = cotangent.astype(jnp.float32)
    grad_mlp_sum, grad_gain3, grad_bias3 = norm_pull(mlp_sum, ln_gain[3], ln_bias[3], grad_result)
    grad_mlp_rows = lax.all_gather(grad_mlp_sum.astype(jnp.bfloat16), "mp", axis=0, tiled=True)
    grad_down = jnp.einsum("tf,te->fe", act_low, grad_mlp_rows, preferred_element_type=jnp.float32)
    grad_act = jnp.einsum("te,fe->tf", grad_mlp_rows, full_down, preferred_element_type=jnp.float32)
    gelu_puller = jax.vjp(lambda values: jax.nn.gelu(values, approximate=True), pre_act)[1]
    grad_pre = gelu_puller(grad_act)[0].astype(jnp.bfloat16)
    grad_up = jnp.einsum("td,tf->df", mlp_input, grad_pre, preferred_element_type=jnp.float32)
    grad_mid_part = jnp.einsum("tf,df->td", grad_pre, full_up, preferred_element_type=jnp.float32)
    grad_mid = lax.psum_scatter(
        grad_mid_part.astype(jnp.bfloat16), "mp", scatter_dimension=0, tiled=True
    ).astype(jnp.float32)
    grad_hidden_norm, grad_gain2, grad_bias2 = norm_pull(
        hidden_state, ln_gain[2], ln_bias[2], grad_mid
    )
    grad_hidden = grad_result + grad_hidden_norm
    grad_attn_sum, grad_gain1, grad_bias1 = norm_pull(attn_sum, ln_gain[1], ln_bias[1], grad_hidden)
    grad_attn_rows = lax.all_gather(grad_attn_sum.astype(jnp.bfloat16), "mp", axis=0, tiled=True)
    grad_outproj = jnp.einsum(
        "tc,te->ce", mixed_heads, grad_attn_rows, preferred_element_type=jnp.float32
    )
    grad_mixed = jnp.einsum(
        "te,ce->tc", grad_attn_rows, full_out, preferred_element_type=jnp.float32
    ).astype(jnp.bfloat16)
    grad_heads = to_heads(grad_mixed)
    again_scores = attention_scores(queries, keys_rot, allowed, scale)
    again_probs = jnp.exp(again_scores - log_total)
    grad_probs = jnp.einsum(
        "hqd,hkd->hqk", grad_heads, values_h, preferred_element_type=jnp.float32
    )
    grad_values = jnp.einsum(
        "hqk,hqd->hkd",
        again_probs.astype(jnp.bfloat16),
        grad_heads,
        preferred_element_type=jnp.float32,
    )
    row_dot = jnp.sum(again_probs * grad_probs, axis=-1, keepdims=True)
    grad_scores = (again_probs * (grad_probs - row_dot) * scale).astype(jnp.bfloat16)
    grad_q_rot = jnp.einsum(
        "hqk,hkd->hqd", grad_scores, keys_rot, preferred_element_type=jnp.float32
    )
    grad_k_rot = jnp.einsum(
        "hqk,hqd->hkd", grad_scores, queries, preferred_element_type=jnp.float32
    )
    zero_heads = jnp.zeros((tok_count, heads_here, HD), jnp.float32)
    unrotate = jax.vjp(lambda values: rotate(values, cos_table, sin_table), zero_heads)[1]
    grad_query = unrotate(jnp.transpose(grad_q_rot, (1, 0, 2)))[0].reshape(
        tok_count, heads_here * HD
    )
    grad_key = unrotate(jnp.transpose(grad_k_rot, (1, 0, 2)))[0].reshape(tok_count, heads_here * HD)
    grad_value = from_heads(grad_values)
    grad_proj = jnp.stack(
        [
            grad_query.astype(jnp.bfloat16),
            grad_key.astype(jnp.bfloat16),
            grad_value.astype(jnp.bfloat16),
        ]
    )
    grad_qkv = jnp.einsum("td,cte->cde", normed_in, grad_proj, preferred_element_type=jnp.float32)
    grad_in_part = jnp.einsum(
        "cte,cde->td", grad_proj, full_qkv, preferred_element_type=jnp.float32
    )
    grad_in = lax.psum_scatter(
        grad_in_part.astype(jnp.bfloat16), "mp", scatter_dimension=0, tiled=True
    ).astype(jnp.float32)
    grad_norm_in, grad_gain0, grad_bias0 = norm_pull(resid_in, ln_gain[0], ln_bias[0], grad_in)
    grad_tokens = grad_hidden + grad_norm_in
    gain_grads = jnp.stack([grad_gain0, grad_gain1, grad_gain2, grad_gain3])
    bias_grads = jnp.stack([grad_bias0, grad_bias1, grad_bias2, grad_bias3])
    gain_grads, bias_grads = (
        lax.psum(gain_grads.astype(jnp.bfloat16), "mp").astype(jnp.float32),
        lax.psum(bias_grads.astype(jnp.bfloat16), "mp").astype(jnp.float32),
    )
    grad_qkv, grad_outproj, grad_up, grad_down, gain_grads, bias_grads = (
        lax.psum_scatter(
            grad_qkv.astype(jnp.bfloat16), "dp", scatter_dimension=1, tiled=True
        ).astype(jnp.float32),
        lax.psum_scatter(
            grad_outproj.astype(jnp.bfloat16), "dp", scatter_dimension=1, tiled=True
        ).astype(jnp.float32),
        lax.psum_scatter(
            grad_up.astype(jnp.bfloat16), "dp", scatter_dimension=0, tiled=True
        ).astype(jnp.float32),
        lax.psum_scatter(
            grad_down.astype(jnp.bfloat16), "dp", scatter_dimension=1, tiled=True
        ).astype(jnp.float32),
        lax.psum_scatter(
            gain_grads.astype(jnp.bfloat16), "dp", scatter_dimension=1, tiled=True
        ).astype(jnp.float32),
        lax.psum_scatter(
            bias_grads.astype(jnp.bfloat16), "dp", scatter_dimension=1, tiled=True
        ).astype(jnp.float32),
    )
    return (output, grad_tokens, grad_qkv, grad_outproj, grad_up, grad_down, gain_grads, bias_grads)


def solution(mesh):
    placed = (
        P("dp", None),
        P("dp"),
        P(),
        P(),
        P(None, "dp", "mp"),
        P("mp", "dp"),
        P("dp", "mp"),
        P("mp", "dp"),
        P(("dp", "mp"), None),
    )
    n_dp, n_mp = mesh.shape["dp"], mesh.shape["mp"]

    def layer(tokens, *rest):
        if n_mp == 2 and tokens.shape[1] == n_dp * LANES // 2:
            return per_device(n_dp, tokens, *rest)
        return plain_device(tokens, *rest)

    return jax.shard_map(
        layer,
        mesh=mesh,
        in_specs=placed,
        out_specs=(
            P(("dp", "mp"), None),
            P(("dp", "mp"), None),
            P(None, "dp", "mp"),
            P("mp", "dp"),
            P("dp", "mp"),
            P("mp", "dp"),
            P(None, "dp"),
            P(None, "dp"),
        ),
        check_vma=False,
    )
```

profile of v0, /device:TPU:0, one launch (start us, length us, event | category | flops | bytes accessed | tf_op | source)
XLA Modules:
  0.0 202.8 jit_solution(16469990444762601757)
XLA Ops:
  2.7 3.0 %collective-permute-start.3 = (bf16[64,2048]{1,0:T(8,128)(2,1)S(1)}, bf16[64,2048]{1,0:T(8,128)(2,1)S(1)}, u32[]{:S(2)}, u32[]{:S(2)}) collective-permute-start(bf16[64,2048]{1,0:T(8,128)(2,1)S(1)} %stage.4.refs_0_), channel_id=1, source_target_pairs={{0,4},{2,6},{8,0},{10,2},{16,8},{18,10},{24,16},{26,18},{28,24},{3... | collective-permute-start | bytes 786440 | tf_op jit(solution)/shard_map/ppermute | solution.py:918
  7.9 4.2 %collective-permute-done.3.refs_2_ = bf16[64,2048]{1,0:T(8,128)(2,1)S(1)} collective-permute-done((bf16[64,2048]{1,0:T(8,128)(2,1)S(1)}, bf16[64,2048]{1,0:T(8,128)(2,1)S(1)}, u32[]{:S(2)}, u32[]{:S(2)}) %collective-permute-start.3) | collective-permute-done | bytes 262176 | tf_op jit(solution)/shard_map/ppermute | solution.py:918
  12.1 1.7 collective-permute-start.5
  14.1 1.7 collective-permute-start.4
  17.2 2.4 %prepare.1 = (bf16[512,1024]{1,0:T(8,128)(2,1)S(1)}, bf16[512,1024]{1,0:T(8,128)(2,1)S(1)}, f32[4,1024]{1,0:T(4,128)S(1)}, f32[4,1024]{1,0:T(4,128)S(1)}) custom-call(s32[2]{0:T(128)S(1)} %pad_add_fusion.ids_ref, bf16[512,1024]{1,0:T(8,128)(2,1)S(1)} %copy-done, f32[4,1024]{1,0:T(4,128)S(1)} %copy-done.6, f32[4,1024]{1,0:T(4,128)S(1)} %copy-done.7), custom_call_target="tpu_custom_call" | custom-call | bytes 12177000 | tf_op jit(solution)/shard_map/prepare/pallas_call | solution.py:76
  19.6 1.5 collective-permute-start.6
  21.7 4.4 %collective-permute-done.6.down_ref.refs_6_ = bf16[64,2048]{1,0:T(8,128)(2,1)S(1)} collective-permute-done((bf16[64,2048]{1,0:T(8,128)(2,1)S(1)}, bf16[64,2048]{1,0:T(8,128)(2,1)S(1)}, u32[]{:S(2)}, u32[]{:S(2)}) %collective-permute-start.6) | collective-permute-done | bytes 262176 | tf_op jit(solution)/shard_map/ppermute | solution.py:918
  29.8 1.7 collective-permute-start.10
  31.8 4.7 %collective-permute-done.10.refs_8_ = bf16[32,2048]{1,0:T(8,128)(2,1)S(1)} collective-permute-done((bf16[32,2048]{1,0:T(8,128)(2,1)S(1)}, bf16[32,2048]{1,0:T(8,128)(2,1)S(1)}, u32[]{:S(2)}, u32[]{:S(2)}) %collective-permute-start.10) | collective-permute-done | bytes 131104 | tf_op jit(solution)/shard_map/ppermute | solution.py:918
  42.7 1.6 rotary.1
  44.3 2.0 qkv_project.1.q_ref
  46.2 2.5 %attend0.1 = (bf16[8,256,256]{2,1,0:T(8,128)(2,1)S(1)}, bf16[256,512]{1,0:T(8,128)(2,1)S(1)}, bf16[256,1024]{1,0:T(8,128)(2,1)S(1)}) custom-call(s32[4]{0:T(128)S(1)} %copy-done.8, bf16[512,1536]{1,0:T(8,128)(2,1)S(1)} %qkv_project.1.q_ref, bf16[512,2048]{1,0:T(8,128)(2,1)S(1)} %assemble.3.refs_0_, bf16[512,2048]{1,0:T(8,128)(2,1)S(1)} %collective-permute-done.13.refs_1_), custom_call_target="tpu_custom_call" | custom-call | bytes 9225000 | tf_op jit(solution)/shard_map/attend0/pallas_call | solution.py:76
  48.8 1.6 collective-permute-start.18
  52.4 4.4 %attend1.1 = (bf16[8,256,512]{2,1,0:T(8,128)(2,1)S(1)}, bf16[256,512]{1,0:T(8,128)(2,1)S(1)}, bf16[256,1024]{1,0:T(8,128)(2,1)S(1)}) custom-call(s32[4]{0:T(128)S(1)} %copy-done.8, bf16[512,1536]{1,0:T(8,128)(2,1)S(1)} %qkv_project.1.q_ref, bf16[512,2048]{1,0:T(8,128)(2,1)S(1)} %assemble.3.refs_0_, bf16[512,2048]{1,0:T(8,128)(2,1)S(1)} %collective-permute-done.13.refs_1_), custom_call_target="tpu_custom_call" | custom-call | bytes 16236000 | tf_op jit(solution)/shard_map/attend1/pallas_call | solution.py:76
  60.9 5.7 %collective-permute-done.17.down_ref.refs_6_ = bf16[64,2048]{1,0:T(8,128)(2,1)S(1)} collective-permute-done((bf16[64,2048]{1,0:T(8,128)(2,1)S(1)}, bf16[64,2048]{1,0:T(8,128)(2,1)S(1)}, u32[]{:S(2)}, u32[]{:S(2)}) %collective-permute-start.17) | collective-permute-done | bytes 262176 | tf_op jit(solution)/shard_map/ppermute | solution.py:918
  66.6 1.6 collective-permute-start.24
  68.2 1.6 collective-permute-start.19
  70.3 4.1 %collective-permute-done.19.refs_7_ = bf16[32,2048]{1,0:T(8,128)(2,1)S(1)} collective-permute-done((bf16[32,2048]{1,0:T(8,128)(2,1)S(1)}, bf16[32,2048]{1,0:T(8,128)(2,1)S(1)}, u32[]{:S(2)}, u32[]{:S(2)}) %collective-permute-start.19) | collective-permute-done | bytes 131104 | tf_op jit(solution)/shard_map/ppermute | solution.py:917
  75.4 1.5 collective-permute-start.27
  77.5 2.9 %collective-permute-done.27.refs_7_ = bf16[32,2048]{1,0:T(8,128)(2,1)S(1)} collective-permute-done((bf16[32,2048]{1,0:T(8,128)(2,1)S(1)}, bf16[32,2048]{1,0:T(8,128)(2,1)S(1)}, u32[]{:S(2)}, u32[]{:S(2)}) %collective-permute-start.27) | collective-permute-done | bytes 131104 | tf_op jit(solution)/shard_map/ppermute | solution.py:917
  83.5 2.6 %up_project.2 = (bf16[256,2048]{1,0:T(8,128)(2,1)S(1)}, bf16[256,2048]{1,0:T(8,128)(2,1)S(1)}) custom-call(bf16[256,1024]{1,0:T(8,128)(2,1)S(1)} %mid_norm.2.a3_ref.refs_0_, bf16[512,2048]{1,0:T(8,128)(2,1)S(1)} %assemble.4.refs_0_.refs_2_, bf16[512,2048]{1,0:T(8,128)(2,1)S(1)} %collective-permute-done.21.refs_1_.refs_3_), custom_call_target="tpu_custom_call" | custom-call | bytes 15867000 | tf_op jit(solution)/shard_map/up_project/pallas_call | solution.py:76
  88.0 1.6 collective-permute-start.30
  90.5 2.6 %up_project.3 = (bf16[256,2048]{1,0:T(8,128)(2,1)S(1)}, bf16[256,2048]{1,0:T(8,128)(2,1)S(1)}) custom-call(bf16[256,1024]{1,0:T(8,128)(2,1)S(1)} %mid_norm.3.a3_ref.refs_1_, bf16[512,2048]{1,0:T(8,128)(2,1)S(1)} %assemble.4.refs_0_.refs_2_, bf16[512,2048]{1,0:T(8,128)(2,1)S(1)} %collective-permute-done.21.refs_1_.refs_3_), custom_call_target="tpu_custom_call" | custom-call | bytes 15867000 | tf_op jit(solution)/shard_map/up_project/pallas_call | solution.py:76
  95.0 7.8 %collective-permute-done.30.zb_ref.refs_5_ = bf16[256,1024]{1,0:T(8,128)(2,1)S(1)} collective-permute-done((bf16[256,1024]{1,0:T(8,128)(2,1)S(1)}, bf16[256,1024]{1,0:T(8,128)(2,1)S(1)}, u32[]{:S(2)}, u32[]{:S(2)}) %collective-permute-start.30) | collective-permute-done | bytes 524320 | tf_op jit(solution)/shard_map/ppermute | solution.py:971
  102.9 3.8 %mlp_back.2 = (bf16[256,1024]{1,0:T(8,128)(2,1)S(1)}, bf16[256,2048]{1,0:T(8,128)(2,1)S(1)}, bf16[256,1024]{1,0:T(8,128)(2,1)S(1)}) custom-call(bf16[256,1024]{1,0:T(8,128)(2,1)S(1)} %down_project.2.za_ref.refs_4_, bf16[256,1024]{1,0:T(8,128)(2,1)S(1)} %collective-permute-done.30.zb_ref.refs_5_, bf16[512,1024]{1,0:T(8,128)(2,1)S(1)} %cotangent_rows.1.cot_ref, ...), custom_call_target="tpu_custom_call" | custom-call | bytes 19926000 | tf_op jit(solution)/shard_map/mlp_back/pallas_call | solution.py:76
  106.6 1.6 collective-permute-start.34
  108.2 5.9 %collective-permute-done.31.zb_ref.refs_7_ = bf16[256,1024]{1,0:T(8,128)(2,1)S(1)} collective-permute-done((bf16[256,1024]{1,0:T(8,128)(2,1)S(1)}, bf16[256,1024]{1,0:T(8,128)(2,1)S(1)}, u32[]{:S(2)}, u32[]{:S(2)}) %collective-permute-start.31) | collective-permute-done | bytes 524320 | tf_op jit(solution)/shard_map/ppermute | solution.py:971
  114.1 3.8 %mlp_back.3 = (bf16[256,1024]{1,0:T(8,128)(2,1)S(1)}, bf16[256,2048]{1,0:T(8,128)(2,1)S(1)}, bf16[256,1024]{1,0:T(8,128)(2,1)S(1)}) custom-call(bf16[256,1024]{1,0:T(8,128)(2,1)S(1)} %down_project.3.za_ref.refs_6_, bf16[256,1024]{1,0:T(8,128)(2,1)S(1)} %collective-permute-done.31.zb_ref.refs_7_, bf16[512,1024]{1,0:T(8,128)(2,1)S(1)} %cotangent_rows.1.cot_ref, ...), custom_call_target="tpu_custom_call" | custom-call | bytes 19926000 | tf_op jit(solution)/shard_map/mlp_back/pallas_call | solution.py:76
  117.9 1.6 weight_grad.6
  119.6 1.6 weight_grad.7
  121.7 1.6 weight_grad.8
  123.4 1.6 weight_grad.9
  127.8 1.7 collective-permute-start.37
  129.6 2.3 %mid_back.2 = (f32[256,1024]{1,0:T(8,128)S(1)}, bf16[256,1024]{1,0:T(8,128)(2,1)S(1)}, bf16[256,512]{1,0:T(8,128)(2,1)S(1)}, f32[4,8,1024]{2,1,0:T(8,128)S(1)}) custom-call(bf16[512,1024]{1,0:T(8,128)(2,1)S(1)} %get-tuple-element.190.x_ref, bf16[256,1024]{1,0:T(8,128)(2,1)S(1)} %get-tuple-element.138.ya_ref.refs_0_, ...), custom_call_target="tpu_custom_call" | custom-call | bytes 12177000 | tf_op jit(solution)/shard_map/mid_back/pallas_call | solution.py:76
  131.9 3.3 %last_norm.1 = (bf16[256,1024]{1,0:T(8,128)(2,1)}, f32[2,8,1024]{2,1,0:T(8,128)S(1)}) custom-call(s32[2]{0:T(128)S(1)} %pad_add_fusion.ids_ref, bf16[512,1024]{1,0:T(8,128)(2,1)S(1)} %get-tuple-element.190.x_ref, bf16[512,1024]{1,0:T(8,128)(2,1)S(1)} %cotangent_rows.1.cot_ref, f32[4,1024]{1,0:T(4,128)S(1)} %get-tuple-element.149.gain_ref, ...), custom_call_target="tpu_custom_call" | custom-call | bytes 11070000 | tf_op jit(solution)/shard_map/last_norm/pallas_call | solution.py:76
  137.7 1.8 collective-permute-done.39.eb_ref
  139.5 2.3 %mid_back.3 = (f32[256,1024]{1,0:T(8,128)S(1)}, bf16[256,1024]{1,0:T(8,128)(2,1)S(1)}, bf16[256,512]{1,0:T(8,128)(2,1)S(1)}, f32[4,8,1024]{2,1,0:T(8,128)S(1)}) custom-call(bf16[512,1024]{1,0:T(8,128)(2,1)S(1)} %get-tuple-element.190.x_ref, bf16[256,1024]{1,0:T(8,128)(2,1)S(1)} %get-tuple-element.141.ya_ref.refs_2_, ...), custom_call_target="tpu_custom_call" | custom-call | bytes 12177000 | tf_op jit(solution)/shard_map/mid_back/pallas_call | solution.py:76
  141.9 5.9 %attend_back.1.refs_1_.g_ref = bf16[512,1536]{1,0:T(8,128)(2,1)S(1)} custom-call(bf16[512,1536]{1,0:T(8,128)(2,1)S(1)} %qkv_project.1.q_ref, bf16[8,256,256]{2,1,0:T(8,128)(2,1)S(1)} %get-tuple-element.178.p0_ref, bf16[8,256,512]{2,1,0:T(8,128)(2,1)S(1)} %get-tuple-element.179.p1_ref, bf16[256,512]{1,0:T(8,128)(2,1)S(1)} %get-tuple-element.180.o0.refs_4_, ...), custom_call_target="tpu_custom_call" | custom-call | bytes 18450000 | tf_op jit(solution)/shard_map/attend_back/pallas_call | solution.py:76
  151.8 1.6 collective-permute-start.46
  153.4 3.6 %in_back.1 = (bf16[256,1024]{1,0:T(8,128)(2,1)S(1)}, bf16[256,1024]{1,0:T(8,128)(2,1)S(1)}, f32[2,8,1024]{2,1,0:T(8,128)S(1)}) custom-call(s32[2]{0:T(128)S(1)} %pad_add_fusion.ids_ref, bf16[512,1536]{1,0:T(8,128)(2,1)S(1)} %attend_back.1.refs_1_.g_ref, bf16[512,1024]{1,0:T(8,128)(2,1)S(1)} %get-tuple-element.190.x_ref, ...), custom_call_target="tpu_custom_call" | custom-call | bytes 13284000 | tf_op jit(solution)/shard_map/in_back/pallas_call | solution.py:76
  157.2 1.6 collective-permute-start.44
  166.9 2.1 %collective-permute-done.50.refs_5_ = bf16[32,2176]{1,0:T(8,128)(2,1)S(1)} collective-permute-done((bf16[32,2176]{1,0:T(8,128)(2,1)S(1)}, bf16[32,2176]{1,0:T(8,128)(2,1)S(1)}, u32[]{:S(2)}, u32[]{:S(2)}) %collective-permute-start.50) | collective-permute-done | bytes 139296 | tf_op jit(solution)/shard_map/ppermute | solution.py:950
  173.8 2.6 %collective-permute-done.51.got_ref = bf16[256,1024]{1,0:T(8,128)(2,1)S(1)} collective-permute-done((bf16[256,1024]{1,0:T(8,128)(2,1)S(1)}, bf16[256,1024]{1,0:T(8,128)(2,1)S(1)}, u32[]{:S(2)}, u32[]{:S(2)}) %collective-permute-start.51) | collective-permute-done | bytes 524320 | tf_op jit(solution)/shard_map/ppermute | solution.py:971
  176.4 2.8 %tokens_back.1 = f32[256,1024]{1,0:T(8,128)} custom-call(s32[2]{0:T(128)S(1)} %pad_add_fusion.ids_ref, bf16[512,1024]{1,0:T(8,128)(2,1)S(1)} %get-tuple-element.190.x_ref, bf16[256,1024]{1,0:T(8,128)(2,1)S(1)} %get-tuple-element.213.keep_ref, bf16[256,1024]{1,0:T(8,128)(2,1)S(1)} %collective-permute-done.51.got_ref, ...), custom_call_target="tpu_custom_call" | custom-call | bytes 14391000 | tf_op jit(solution)/shard_map/tokens_back/pallas_call | solution.py:76
  181.6 9.8 %collective-permute-done.52.refs_8_ = bf16[64,4096]{1,0:T(8,128)(2,1)S(1)} collective-permute-done((bf16[64,4096]{1,0:T(8,128)(2,1)S(1)}, bf16[64,4096]{1,0:T(8,128)(2,1)S(1)}, u32[]{:S(2)}, u32[]{:S(2)}) %collective-permute-start.52) | collective-permute-done | bytes 524320 | tf_op jit(solution)/shard_map/ppermute | solution.py:950
  192.5 1.8 collective-permute-done.58.refs_5_
  195.1 1.5 collective-permute-start.57
  196.7 4.8 %collective-permute-done.59.refs_6_ = bf16[64,2176]{1,0:T(8,128)(2,1)S(1)} collective-permute-done((bf16[64,2176]{1,0:T(8,128)(2,1)S(1)}, bf16[64,2176]{1,0:T(8,128)(2,1)S(1)}, u32[]{:S(2)}, u32[]{:S(2)}) %collective-permute-start.59) | collective-permute-done | bytes 278560 | tf_op jit(solution)/shard_map/ppermute | solution.py:950
  (146 shorter events, 60.9 us)
Async XLA Ops:
  2.7 9.4 %collective-permute-start.3 = (bf16[64,2048]{1,0:T(8,128)(2,1)S(1)}, bf16[64,2048]{1,0:T(8,128)(2,1)S(1)}, u32[]{:S(2)}, u32[]{:S(2)}) collective-permute-start(bf16[64,2048]{1,0:T(8,128)(2,1)S(1)} %stage.4.refs_0_), channel_id=1, source_target_pairs={{0,4},{2,6},{8,0},{10,2},{16,8},{18,10},{24,16},{26,18},{28,24},{3... | collective-permute-start | bytes 786440 | tf_op jit(solution)/shard_map/ppermute | solution.py:918
  5.7 8.0 %collective-permute-start = (bf16[64,2048]{1,0:T(8,128)(2,1)S(1)}, bf16[64,2048]{1,0:T(8,128)(2,1)S(1)}, u32[]{:S(2)}, u32[]{:S(2)}) collective-permute-start(bf16[64,2048]{1,0:T(8,128)(2,1)S(1)} %stage.4.refs_0_), channel_id=1, source_target_pairs={{0,8},{2,10},{8,16},{10,18},{16,24},{18,26},{24,28},{26,30},{28,20... | collective-permute-start | bytes 786440 | tf_op jit(solution)/shard_map/ppermute | solution.py:917
  12.1 7.6 %collective-permute-start.5 = (bf16[64,2048]{1,0:T(8,128)(2,1)S(1)}, bf16[64,2048]{1,0:T(8,128)(2,1)S(1)}, u32[]{:S(2)}, u32[]{:S(2)}) collective-permute-start(bf16[64,2048]{1,0:T(8,128)(2,1)S(1)} %collective-permute-done.3.refs_2_), channel_id=1, source_target_pairs={{0,4},{2,6},{8,0},{10,2},{16,8},{18,10},{24,16},{26,18},{28,24},{3... | collective-permute-start | bytes 786440 | tf_op jit(solution)/shard_map/ppermute | solution.py:918
  13.7 7.5 %collective-permute-start.1 = (bf16[64,2048]{1,0:T(8,128)(2,1)S(1)}, bf16[64,2048]{1,0:T(8,128)(2,1)S(1)}, u32[]{:S(2)}, u32[]{:S(2)}) collective-permute-start(bf16[64,2048]{1,0:T(8,128)(2,1)S(1)} %collective-permute-done.refs_1_), channel_id=1, source_target_pairs={{0,8},{2,10},{8,16},{10,18},{16,24},{18,26},{24,28},{26,30},{28,20... | collective-permute-start | bytes 786440 | tf_op jit(solution)/shard_map/ppermute | solution.py:917
  14.1 12.8 %collective-permute-start.4 = (bf16[256,1024]{1,0:T(8,128)(2,1)}, bf16[256,1024]{1,0:T(8,128)(2,1)S(1)}, u32[]{:S(2)}, u32[]{:S(2)}) collective-permute-start(bf16[256,1024]{1,0:T(8,128)(2,1)} %own_ref.1), channel_id=1, source_target_pairs={{0,1},{1,0},{2,3},{3,2},{4,5},{5,4},{6,7},{7,6},{8,9},{9,8},{10,11... | collective-permute-start | bytes 1572872 | tf_op jit(solution)/shard_map/ppermute | solution.py:971
  19.6 6.5 %collective-permute-start.6 = (bf16[64,2048]{1,0:T(8,128)(2,1)S(1)}, bf16[64,2048]{1,0:T(8,128)(2,1)S(1)}, u32[]{:S(2)}, u32[]{:S(2)}) collective-permute-start(bf16[64,2048]{1,0:T(8,128)(2,1)S(1)} %collective-permute-done.5.refs_4_), channel_id=1, source_target_pairs={{0,4},{2,6},{8,0},{10,2},{16,8},{18,10},{24,16},{26,18},{28,24},{3... | collective-permute-start | bytes 786440 | tf_op jit(solution)/shard_map/ppermute | solution.py:918
  21.2 6.5 %collective-permute-start.2 = (bf16[64,2048]{1,0:T(8,128)(2,1)S(1)}, bf16[64,2048]{1,0:T(8,128)(2,1)S(1)}, u32[]{:S(2)}, u32[]{:S(2)}) collective-permute-start(bf16[64,2048]{1,0:T(8,128)(2,1)S(1)} %collective-permute-done.1.refs_3_), channel_id=1, source_target_pairs={{0,8},{2,10},{8,16},{10,18},{16,24},{18,26},{24,28},{26,30},{28,20... | collective-permute-start | bytes 786440 | tf_op jit(solution)/shard_map/ppermute | solution.py:917
  27.7 9.4 %collective-permute-start.7 = (bf16[64,2048]{1,0:T(8,128)(2,1)S(1)}, bf16[64,2048]{1,0:T(8,128)(2,1)S(1)}, u32[]{:S(2)}, u32[]{:S(2)}) collective-permute-start(bf16[64,2048]{1,0:T(8,128)(2,1)S(1)} %stage.3.refs_0_), channel_id=1, source_target_pairs={{0,8},{2,10},{8,16},{10,18},{16,24},{18,26},{24,28},{26,30},{28,20... | collective-permute-start | bytes 786440 | tf_op jit(solution)/shard_map/ppermute | solution.py:917
  28.4 8.8 %collective-permute-start.8 = (bf16[64,2048]{1,0:T(8,128)(2,1)S(1)}, bf16[64,2048]{1,0:T(8,128)(2,1)S(1)}, u32[]{:S(2)}, u32[]{:S(2)}) collective-permute-start(bf16[64,2048]{1,0:T(8,128)(2,1)S(1)} %stage.3.refs_0_), channel_id=1, source_target_pairs={{0,4},{2,6},{8,0},{10,2},{16,8},{18,10},{24,16},{26,18},{28,24},{3... | collective-permute-start | bytes 786440 | tf_op jit(solution)/shard_map/ppermute | solution.py:918
  29.8 6.8 %collective-permute-start.10 = (bf16[32,2048]{1,0:T(8,128)(2,1)S(1)}, bf16[32,2048]{1,0:T(8,128)(2,1)S(1)}, u32[]{:S(2)}, u32[]{:S(2)}) collective-permute-start(bf16[32,2048]{1,0:T(8,128)(2,1)S(1)} %get-tuple-element.128), channel_id=1, source_target_pairs={{0,4},{2,6},{8,0},{10,2},{16,8},{18,10},{24,16},{26,18},{28,24},{3... | collective-permute-start | bytes 393224 | tf_op jit(solution)/shard_map/ppermute | solution.py:918
  37.2 7.1 %collective-permute-start.13 = (bf16[512,2048]{1,0:T(8,128)(2,1)S(1)}, bf16[512,2048]{1,0:T(8,128)(2,1)S(1)}, u32[]{:S(2)}, u32[]{:S(2)}) collective-permute-start(bf16[512,2048]{1,0:T(8,128)(2,1)S(1)} %assemble.3.refs_0_), channel_id=1, source_target_pairs={{0,2},{2,0},{4,6},{6,4},{8,10},{10,8},{12,14},{14,12},{16,18},{18,... | collective-permute-start | bytes 6291464 | tf_op jit(solution)/shard_map/ppermute | solution.py:895
  37.3 13.1 %collective-permute-start.15 = (bf16[64,2048]{1,0:T(8,128)(2,1)S(1)}, bf16[64,2048]{1,0:T(8,128)(2,1)S(1)}, u32[]{:S(2)}, u32[]{:S(2)}) collective-permute-start(bf16[64,2048]{1,0:T(8,128)(2,1)S(1)} %stage.5.refs_0_), channel_id=1, source_target_pairs={{0,4},{2,6},{8,0},{10,2},{16,8},{18,10},{24,16},{26,18},{28,24},{3... | collective-permute-start | bytes 786440 | tf_op jit(solution)/shard_map/ppermute | solution.py:918
  38.8 12.8 %collective-permute-start.14 = (bf16[64,2048]{1,0:T(8,128)(2,1)S(1)}, bf16[64,2048]{1,0:T(8,128)(2,1)S(1)}, u32[]{:S(2)}, u32[]{:S(2)}) collective-permute-start(bf16[64,2048]{1,0:T(8,128)(2,1)S(1)} %stage.5.refs_0_), channel_id=1, source_target_pairs={{0,8},{2,10},{8,16},{10,18},{16,24},{18,26},{24,28},{26,30},{28,20... | collective-permute-start | bytes 786440 | tf_op jit(solution)/shard_map/ppermute | solution.py:917
  39.3 17.4 %collective-permute-start.12 = (bf16[64,2048]{1,0:T(8,128)(2,1)S(1)}, bf16[64,2048]{1,0:T(8,128)(2,1)S(1)}, u32[]{:S(2)}, u32[]{:S(2)}) collective-permute-start(bf16[64,2048]{1,0:T(8,128)(2,1)S(1)} %collective-permute-done.8.refs_2_), channel_id=1, source_target_pairs={{0,4},{2,6},{8,0},{10,2},{16,8},{18,10},{24,16},{26,18},{28,24},{3... | collective-permute-start | bytes 786440 | tf_op jit(solution)/shard_map/ppermute | solution.py:918
  40.8 16.6 %collective-permute-start.11 = (bf16[64,2048]{1,0:T(8,128)(2,1)S(1)}, bf16[64,2048]{1,0:T(8,128)(2,1)S(1)}, u32[]{:S(2)}, u32[]{:S(2)}) collective-permute-start(bf16[64,2048]{1,0:T(8,128)(2,1)S(1)} %collective-permute-done.7.refs_1_), channel_id=1, source_target_pairs={{0,8},{2,10},{8,16},{10,18},{16,24},{18,26},{24,28},{26,30},{28,20... | collective-permute-start | bytes 786440 | tf_op jit(solution)/shard_map/ppermute | solution.py:917
  48.8 19.4 %collective-permute-start.18 = (bf16[256,1024]{1,0:T(8,128)(2,1)S(1)}, bf16[256,1024]{1,0:T(8,128)(2,1)S(1)}, u32[]{:S(2)}, u32[]{:S(2)}) collective-permute-start(bf16[256,1024]{1,0:T(8,128)(2,1)S(1)} %get-tuple-element.138.ya_ref.refs_0_), channel_id=1, source_target_pairs={{0,1},{1,0},{2,3},{3,2},{4,5},{5,4},{6,7},{7,6},{8,9},{9,8},{10,11... | collective-permute-start | bytes 1572872 | tf_op jit(solution)/shard_map/ppermute | solution.py:971
  50.3 8.5 %collective-permute-start.23 = (bf16[64,2048]{1,0:T(8,128)(2,1)S(1)}, bf16[64,2048]{1,0:T(8,128)(2,1)S(1)}, u32[]{:S(2)}, u32[]{:S(2)}) collective-permute-start(bf16[64,2048]{1,0:T(8,128)(2,1)S(1)} %collective-permute-done.15.refs_2_), channel_id=1, source_target_pairs={{0,4},{2,6},{8,0},{10,2},{16,8},{18,10},{24,16},{26,18},{28,24},{3... | collective-permute-start | bytes 786440 | tf_op jit(solution)/shard_map/ppermute | solution.py:918
  51.6 7.8 %collective-permute-start.22 = (bf16[64,2048]{1,0:T(8,128)(2,1)S(1)}, bf16[64,2048]{1,0:T(8,128)(2,1)S(1)}, u32[]{:S(2)}, u32[]{:S(2)}) collective-permute-start(bf16[64,2048]{1,0:T(8,128)(2,1)S(1)} %collective-permute-done.14.refs_1_), channel_id=1, source_target_pairs={{0,8},{2,10},{8,16},{10,18},{16,24},{18,26},{24,28},{26,30},{28,20... | collective-permute-start | bytes 786440 | tf_op jit(solution)/shard_map/ppermute | solution.py:917
  56.8 18.6 %collective-permute-start.26 = (bf16[256,1024]{1,0:T(8,128)(2,1)S(1)}, bf16[256,1024]{1,0:T(8,128)(2,1)S(1)}, u32[]{:S(2)}, u32[]{:S(2)}) collective-permute-start(bf16[256,1024]{1,0:T(8,128)(2,1)S(1)} %get-tuple-element.141.ya_ref.refs_2_), channel_id=1, source_target_pairs={{0,1},{1,0},{2,3},{3,2},{4,5},{5,4},{6,7},{7,6},{8,9},{9,8},{10,11... | collective-permute-start | bytes 1572872 | tf_op jit(solution)/shard_map/ppermute | solution.py:971
  57.4 9.2 %collective-permute-start.17 = (bf16[64,2048]{1,0:T(8,128)(2,1)S(1)}, bf16[64,2048]{1,0:T(8,128)(2,1)S(1)}, u32[]{:S(2)}, u32[]{:S(2)}) collective-permute-start(bf16[64,2048]{1,0:T(8,128)(2,1)S(1)} %collective-permute-done.12.refs_4_), channel_id=1, source_target_pairs={{0,4},{2,6},{8,0},{10,2},{16,8},{18,10},{24,16},{26,18},{28,24},{3... | collective-permute-start | bytes 786440 | tf_op jit(solution)/shard_map/ppermute | solution.py:918
  58.8 9.4 %collective-permute-start.16 = (bf16[64,2048]{1,0:T(8,128)(2,1)S(1)}, bf16[64,2048]{1,0:T(8,128)(2,1)S(1)}, u32[]{:S(2)}, u32[]{:S(2)}) collective-permute-start(bf16[64,2048]{1,0:T(8,128)(2,1)S(1)} %collective-permute-done.11.refs_3_), channel_id=1, source_target_pairs={{0,8},{2,10},{8,16},{10,18},{16,24},{18,26},{24,28},{26,30},{28,20... | collective-permute-start | bytes 786440 | tf_op jit(solution)/shard_map/ppermute | solution.py:917
  59.4 16.0 %collective-permute-start.25 = (bf16[64,2048]{1,0:T(8,128)(2,1)S(1)}, bf16[64,2048]{1,0:T(8,128)(2,1)S(1)}, u32[]{:S(2)}, u32[]{:S(2)}) collective-permute-start(bf16[64,2048]{1,0:T(8,128)(2,1)S(1)} %collective-permute-done.23.refs_4_), channel_id=1, source_target_pairs={{0,4},{2,6},{8,0},{10,2},{16,8},{18,10},{24,16},{26,18},{28,24},{3... | collective-permute-start | bytes 786440 | tf_op jit(solution)/shard_map/ppermute | solution.py:918
  66.6 8.8 %collective-permute-start.24 = (bf16[64,2048]{1,0:T(8,128)(2,1)S(1)}, bf16[64,2048]{1,0:T(8,128)(2,1)S(1)}, u32[]{:S(2)}, u32[]{:S(2)}) collective-permute-start(bf16[64,2048]{1,0:T(8,128)(2,1)S(1)} %collective-permute-done.22.refs_3_), channel_id=1, source_target_pairs={{0,8},{2,10},{8,16},{10,18},{16,24},{18,26},{24,28},{26,30},{28,20... | collective-permute-start | bytes 786440 | tf_op jit(solution)/shard_map/ppermute | solution.py:917
  68.2 6.2 %collective-permute-start.19 = (bf16[32,2048]{1,0:T(8,128)(2,1)S(1)}, bf16[32,2048]{1,0:T(8,128)(2,1)S(1)}, u32[]{:S(2)}, u32[]{:S(2)}) collective-permute-start(bf16[32,2048]{1,0:T(8,128)(2,1)S(1)} %get-tuple-element.146), channel_id=1, source_target_pairs={{0,8},{2,10},{8,16},{10,18},{16,24},{18,26},{24,28},{26,30},{28,20... | collective-permute-start | bytes 393224 | tf_op jit(solution)/shard_map/ppermute | solution.py:917
  77.5 6.0 %collective-permute-start.21 = (bf16[512,2048]{1,0:T(8,128)(2,1)S(1)}, bf16[512,2048]{1,0:T(8,128)(2,1)S(1)}, u32[]{:S(2)}, u32[]{:S(2)}) collective-permute-start(bf16[512,2048]{1,0:T(8,128)(2,1)S(1)} %assemble.4.refs_0_.refs_2_), channel_id=1, source_target_pairs={{0,2},{2,0},{4,6},{6,4},{8,10},{10,8},{12,14},{14,12},{16,18},{18,... | collective-permute-start | bytes 6291464 | tf_op jit(solution)/shard_map/ppermute | solution.py:895
  88.0 14.8 %collective-permute-start.30 = (bf16[256,1024]{1,0:T(8,128)(2,1)S(1)}, bf16[256,1024]{1,0:T(8,128)(2,1)S(1)}, u32[]{:S(2)}, u32[]{:S(2)}) collective-permute-start(bf16[256,1024]{1,0:T(8,128)(2,1)S(1)} %down_project.2.za_ref.refs_4_), channel_id=1, source_target_pairs={{0,1},{1,0},{2,3},{3,2},{4,5},{5,4},{6,7},{7,6},{8,9},{9,8},{10,11... | collective-permute-start | bytes 1572872 | tf_op jit(solution)/shard_map/ppermute | solution.py:971
  94.5 19.6 %collective-permute-start.31 = (bf16[256,1024]{1,0:T(8,128)(2,1)S(1)}, bf16[256,1024]{1,0:T(8,128)(2,1)S(1)}, u32[]{:S(2)}, u32[]{:S(2)}) collective-permute-start(bf16[256,1024]{1,0:T(8,128)(2,1)S(1)} %down_project.3.za_ref.refs_6_), channel_id=1, source_target_pairs={{0,1},{1,0},{2,3},{3,2},{4,5},{5,4},{6,7},{7,6},{8,9},{9,8},{10,11... | collective-permute-start | bytes 1572872 | tf_op jit(solution)/shard_map/ppermute | solution.py:971
  106.6 18.5 %collective-permute-start.34 = (bf16[256,1024]{1,0:T(8,128)(2,1)S(1)}, bf16[256,1024]{1,0:T(8,128)(2,1)S(1)}, u32[]{:S(2)}, u32[]{:S(2)}) collective-permute-start(bf16[256,1024]{1,0:T(8,128)(2,1)S(1)} %get-tuple-element.174.ea_ref), channel_id=1, source_target_pairs={{0,1},{1,0},{2,3},{3,2},{4,5},{5,4},{6,7},{7,6},{8,9},{9,8},{10,11... | collective-permute-start | bytes 1572872 | tf_op jit(solution)/shard_map/ppermute | solution.py:971
  125.0 10.2 %collective-permute-start.35 = (bf16[448,2048]{1,0:T(8,128)(2,1)S(1)}, bf16[448,2048]{1,0:T(8,128)(2,1)S(1)}, u32[]{:S(2)}, u32[]{:S(2)}) collective-permute-start(bf16[448,2048]{1,0:T(8,128)(2,1)S(1)} %get-tuple-element.186), channel_id=1, source_target_pairs={{0,2},{2,0},{4,6},{6,4},{8,10},{10,8},{12,14},{14,12},{16,18},{18,... | collective-permute-start | bytes 5505032 | tf_op jit(solution)/shard_map/ppermute | solution.py:895
  125.1 10.1 %collective-permute-start.36 = (bf16[448,2048]{1,0:T(8,128)(2,1)S(1)}, bf16[448,2048]{1,0:T(8,128)(2,1)S(1)}, u32[]{:S(2)}, u32[]{:S(2)}) collective-permute-start(bf16[448,2048]{1,0:T(8,128)(2,1)S(1)} %get-tuple-element.189), channel_id=1, source_target_pairs={{0,2},{2,0},{4,6},{6,4},{8,10},{10,8},{12,14},{14,12},{16,18},{18,... | collective-permute-start | bytes 5505032 | tf_op jit(solution)/shard_map/ppermute | solution.py:895
  125.6 13.9 %collective-permute-start.39 = (bf16[256,1024]{1,0:T(8,128)(2,1)S(1)}, bf16[256,1024]{1,0:T(8,128)(2,1)S(1)}, u32[]{:S(2)}, u32[]{:S(2)}) collective-permute-start(bf16[256,1024]{1,0:T(8,128)(2,1)S(1)} %get-tuple-element.191.ea_ref), channel_id=1, source_target_pairs={{0,1},{1,0},{2,3},{3,2},{4,5},{5,4},{6,7},{7,6},{8,9},{9,8},{10,11... | collective-permute-start | bytes 1572872 | tf_op jit(solution)/shard_map/ppermute | solution.py:971
  127.2 8.1 %collective-permute-start.38 = (bf16[32,4096]{1,0:T(8,128)(2,1)S(1)}, bf16[32,4096]{1,0:T(8,128)(2,1)S(1)}, u32[]{:S(2)}, u32[]{:S(2)}) collective-permute-start(bf16[32,4096]{1,0:T(8,128)(2,1)S(1)} %ring_sum.17), channel_id=1, source_target_pairs={{0,4},{2,6},{8,0},{10,2},{16,8},{18,10},{24,16},{26,18},{28,24},{3... | collective-permute-start | bytes 786440 | tf_op jit(solution)/shard_map/ppermute | solution.py:950
  127.8 8.2 %collective-permute-start.37 = (bf16[32,4096]{1,0:T(8,128)(2,1)S(1)}, bf16[32,4096]{1,0:T(8,128)(2,1)S(1)}, u32[]{:S(2)}, u32[]{:S(2)}) collective-permute-start(bf16[32,4096]{1,0:T(8,128)(2,1)S(1)} %ring_sum.16), channel_id=1, source_target_pairs={{0,8},{2,10},{8,16},{10,18},{16,24},{18,26},{24,28},{26,30},{28,20... | collective-permute-start | bytes 786440 | tf_op jit(solution)/shard_map/ppermute | solution.py:950
  135.4 15.3 %collective-permute-start.41 = (bf16[64,4096]{1,0:T(8,128)(2,1)S(1)}, bf16[64,4096]{1,0:T(8,128)(2,1)S(1)}, u32[]{:S(2)}, u32[]{:S(2)}) collective-permute-start(bf16[64,4096]{1,0:T(8,128)(2,1)S(1)} %ring_sum.19), channel_id=1, source_target_pairs={{0,4},{2,6},{8,0},{10,2},{16,8},{18,10},{24,16},{26,18},{28,24},{3... | collective-permute-start | bytes 1572872 | tf_op jit(solution)/shard_map/ppermute | solution.py:950
  136.2 14.5 %collective-permute-start.40 = (bf16[64,4096]{1,0:T(8,128)(2,1)S(1)}, bf16[64,4096]{1,0:T(8,128)(2,1)S(1)}, u32[]{:S(2)}, u32[]{:S(2)}) collective-permute-start(bf16[64,4096]{1,0:T(8,128)(2,1)S(1)} %ring_sum.18), channel_id=1, source_target_pairs={{0,8},{2,10},{8,16},{10,18},{16,24},{18,26},{24,28},{26,30},{28,20... | collective-permute-start | bytes 1572872 | tf_op jit(solution)/shard_map/ppermute | solution.py:950
  150.7 18.4 %collective-permute-start.48 = (bf16[448,2048]{1,0:T(8,128)(2,1)S(1)}, bf16[448,2048]{1,0:T(8,128)(2,1)S(1)}, u32[]{:S(2)}, u32[]{:S(2)}) collective-permute-start(bf16[448,2048]{1,0:T(8,128)(2,1)S(1)} %get-tuple-element.211), channel_id=1, source_target_pairs={{0,2},{2,0},{4,6},{6,4},{8,10},{10,8},{12,14},{14,12},{16,18},{18,... | collective-permute-start | bytes 5505032 | tf_op jit(solution)/shard_map/ppermute | solution.py:895
  151.0 14.3 %collective-permute-start.47 = (bf16[64,4096]{1,0:T(8,128)(2,1)S(1)}, bf16[64,4096]{1,0:T(8,128)(2,1)S(1)}, u32[]{:S(2)}, u32[]{:S(2)}) collective-permute-start(bf16[64,4096]{1,0:T(8,128)(2,1)S(1)} %ring_sum.21), channel_id=1, source_target_pairs={{0,4},{2,6},{8,0},{10,2},{16,8},{18,10},{24,16},{26,18},{28,24},{3... | collective-permute-start | bytes 1572872 | tf_op jit(solution)/shard_map/ppermute | solution.py:950
  151.8 14.9 %collective-permute-start.46 = (bf16[64,4096]{1,0:T(8,128)(2,1)S(1)}, bf16[64,4096]{1,0:T(8,128)(2,1)S(1)}, u32[]{:S(2)}, u32[]{:S(2)}) collective-permute-start(bf16[64,4096]{1,0:T(8,128)(2,1)S(1)} %ring_sum.20), channel_id=1, source_target_pairs={{0,8},{2,10},{8,16},{10,18},{16,24},{18,26},{24,28},{26,30},{28,20... | collective-permute-start | bytes 1572872 | tf_op jit(solution)/shard_map/ppermute | solution.py:950
  162.1 14.4 %collective-permute-start.51 = (bf16[256,1024]{1,0:T(8,128)(2,1)S(1)}, bf16[256,1024]{1,0:T(8,128)(2,1)S(1)}, u32[]{:S(2)}, u32[]{:S(2)}) collective-permute-start(bf16[256,1024]{1,0:T(8,128)(2,1)S(1)} %get-tuple-element.215), channel_id=1, source_target_pairs={{0,1},{1,0},{2,3},{3,2},{4,5},{5,4},{6,7},{7,6},{8,9},{9,8},{10,11... | collective-permute-start | bytes 1572872 | tf_op jit(solution)/shard_map/ppermute | solution.py:971
  163.3 5.8 %collective-permute-start.50 = (bf16[32,2176]{1,0:T(8,128)(2,1)S(1)}, bf16[32,2176]{1,0:T(8,128)(2,1)S(1)}, u32[]{:S(2)}, u32[]{:S(2)}) collective-permute-start(bf16[32,2176]{1,0:T(8,128)(2,1)S(1)} %ring_sum.23), channel_id=1, source_target_pairs={{0,4},{2,6},{8,0},{10,2},{16,8},{18,10},{24,16},{26,18},{28,24},{3... | collective-permute-start | bytes 417800 | tf_op jit(solution)/shard_map/ppermute | solution.py:950
  169.2 10.1 %collective-permute-start.54 = (bf16[64,2176]{1,0:T(8,128)(2,1)S(1)}, bf16[64,2176]{1,0:T(8,128)(2,1)S(1)}, u32[]{:S(2)}, u32[]{:S(2)}) collective-permute-start(bf16[64,2176]{1,0:T(8,128)(2,1)S(1)} %ring_sum.27), channel_id=1, source_target_pairs={{0,4},{2,6},{8,0},{10,2},{16,8},{18,10},{24,16},{26,18},{28,24},{3... | collective-permute-start | bytes 835592 | tf_op jit(solution)/shard_map/ppermute | solution.py:950
  170.5 9.6 %collective-permute-start.53 = (bf16[64,2176]{1,0:T(8,128)(2,1)S(1)}, bf16[64,2176]{1,0:T(8,128)(2,1)S(1)}, u32[]{:S(2)}, u32[]{:S(2)}) collective-permute-start(bf16[64,2176]{1,0:T(8,128)(2,1)S(1)} %ring_sum.26), channel_id=1, source_target_pairs={{0,8},{2,10},{8,16},{10,18},{16,24},{18,26},{24,28},{26,30},{28,20... | collective-permute-start | bytes 835592 | tf_op jit(solution)/shard_map/ppermute | solution.py:950
  171.8 19.6 %collective-permute-start.52 = (bf16[64,4096]{1,0:T(8,128)(2,1)S(1)}, bf16[64,4096]{1,0:T(8,128)(2,1)S(1)}, u32[]{:S(2)}, u32[]{:S(2)}) collective-permute-start(bf16[64,4096]{1,0:T(8,128)(2,1)S(1)} %ring_sum.24), channel_id=1, source_target_pairs={{0,8},{2,10},{8,16},{10,18},{16,24},{18,26},{24,28},{26,30},{28,20... | collective-permute-start | bytes 1572872 | tf_op jit(solution)/shard_map/ppermute | solution.py:950
  173.3 18.1 %collective-permute-start.55 = (bf16[64,4096]{1,0:T(8,128)(2,1)S(1)}, bf16[64,4096]{1,0:T(8,128)(2,1)S(1)}, u32[]{:S(2)}, u32[]{:S(2)}) collective-permute-start(bf16[64,4096]{1,0:T(8,128)(2,1)S(1)} %ring_sum.25), channel_id=1, source_target_pairs={{0,4},{2,6},{8,0},{10,2},{16,8},{18,10},{24,16},{26,18},{28,24},{3... | collective-permute-start | bytes 1572872 | tf_op jit(solution)/shard_map/ppermute | solution.py:950
  179.3 15.0 %collective-permute-start.58 = (bf16[64,2176]{1,0:T(8,128)(2,1)S(1)}, bf16[64,2176]{1,0:T(8,128)(2,1)S(1)}, u32[]{:S(2)}, u32[]{:S(2)}) collective-permute-start(bf16[64,2176]{1,0:T(8,128)(2,1)S(1)} %ring_sum.29), channel_id=1, source_target_pairs={{0,4},{2,6},{8,0},{10,2},{16,8},{18,10},{24,16},{26,18},{28,24},{3... | collective-permute-start | bytes 835592 | tf_op jit(solution)/shard_map/ppermute | solution.py:950
  180.3 14.8 %collective-permute-start.56 = (bf16[64,2176]{1,0:T(8,128)(2,1)S(1)}, bf16[64,2176]{1,0:T(8,128)(2,1)S(1)}, u32[]{:S(2)}, u32[]{:S(2)}) collective-permute-start(bf16[64,2176]{1,0:T(8,128)(2,1)S(1)} %ring_sum.28), channel_id=1, source_target_pairs={{0,8},{2,10},{8,16},{10,18},{16,24},{18,26},{24,28},{26,30},{28,20... | collective-permute-start | bytes 835592 | tf_op jit(solution)/shard_map/ppermute | solution.py:950
  194.4 7.0 %collective-permute-start.59 = (bf16[64,2176]{1,0:T(8,128)(2,1)S(1)}, bf16[64,2176]{1,0:T(8,128)(2,1)S(1)}, u32[]{:S(2)}, u32[]{:S(2)}) collective-permute-start(bf16[64,2176]{1,0:T(8,128)(2,1)S(1)} %ring_sum.31), channel_id=1, source_target_pairs={{0,4},{2,6},{8,0},{10,2},{16,8},{18,10},{24,16},{26,18},{28,24},{3... | collective-permute-start | bytes 835592 | tf_op jit(solution)/shard_map/ppermute | solution.py:950
  195.1 6.8 %collective-permute-start.57 = (bf16[64,2176]{1,0:T(8,128)(2,1)S(1)}, bf16[64,2176]{1,0:T(8,128)(2,1)S(1)}, u32[]{:S(2)}, u32[]{:S(2)}) collective-permute-start(bf16[64,2176]{1,0:T(8,128)(2,1)S(1)} %ring_sum.30), channel_id=1, source_target_pairs={{0,8},{2,10},{8,16},{10,18},{16,24},{18,26},{24,28},{26,30},{28,20... | collective-permute-start | bytes 835592 | tf_op jit(solution)/shard_map/ppermute | solution.py:950
  (21 other events, 86.9 us)
where the time goes:
time: 203 us
  waiting for transfers between devices  72.2 us (36%)
  Pallas kernels  66.7 us (33%)
  starting transfers between devices  57.5 us (28%)
  local copies, waits for them, and re-layouts  5.18 us (3%)
    pallas_call x49, Pallas kernels, kernel_call(): pl.pallas_call(body, in_specs=[smem()] * smems + [whole()] * (len(args) -...  64.8 us
    ppermute x16, waiting for transfers between devices, step(): came.append(lax.ppermute(sent[way], 'dp', perm))  21.3 us
    ppermute x12, waiting for transfers between devices, step(): self.down = lax.ppermute(down, 'dp', ring.down)  21 us
    ppermute x9, waiting for transfers between devices, swap_sides(): return lax.ppermute(value, 'mp', [(0, 1), (1, 0)])  18.9 us
    ppermute x12, starting transfers between devices, step(): self.down = lax.ppermute(down, 'dp', ring.down)  17.5 us
    ppermute x16, starting transfers between devices, step(): came.append(lax.ppermute(sent[way], 'dp', perm))  16.4 us
    ppermute x9, starting transfers between devices, swap_sides(): return lax.ppermute(value, 'mp', [(0, 1), (1, 0)])  11.8 us
    ppermute x12, starting transfers between devices, step(): self.up = lax.ppermute(up, 'dp', ring.up)  9.22 us
  transfers between devices with their start and end apart: 60, of which 26 were waited for; matrix products, arithmetic and copies ran while one was open for 0% of the time, Pallas kernels for 32%

commit v1 on v0

--- a/solution.py
+++ b/solution.py
@@ -58,16 +58,17 @@
 
 
 ORDER = {
-    "s12": ("stages",), "s13": ("a1",), "s14": ("cot_got",), "s21": ("s14_sent",), "s31": ("s14",),
-    "cot_swap": ("s11",), "w1": ("s21",), "rotary": ("own1",), "cot": ("own1",), "s22": ("own1",),
-    "qkv": ("cot",), "attend1": ("part0", "s31"), "s23": ("part1",), "s24": ("y0",),
-    "norm0": ("own2",), "s34": ("own2", "y1"), "up1": ("down0",), "down1": ("down0",),
-    "back1": ("back0",), "up_other": ("down_other",), "down_mine": ("up_other",),
-    "up_mine": ("down_mine", "down_far"), "up_near": ("da0", "up_mine"), "mid0": ("m1_sent",),
-    "last": ("mid0",), "m2": ("last",), "mid1": ("m2_sent",), "attn_near": ("m2",), "m3": ("attn_other",),
-    "in_back": ("m3_sent",), "attn_mine": ("gain_sum",), "gains": ("attn_mine",),
-    "part_give": ("gains",), "m4": ("q1_sent",), "q2": ("m4_sent",), "tokens": ("q2_sent",),
-    "q3": ("tokens",), "m_end": ("q3_sent",), "q4": ("m_end",),
+    "s12": ("stages",), "s13": ("a1",), "s14": ("cot_got", "s11"), "s21": ("s14_sent",),
+    "s31": ("s14",), "cot_swap": ("s11",), "w1": ("s21",), "rotary": ("own1",), "cot": ("own1",),
+    "s22": ("own1",), "qkv": ("cot",), "attend1": ("part0", "s31"), "s23": ("part1",), "s24": ("y0",),
+    "norm0": ("own2",), "y1": ("s32",), "s34": ("own2",), "own3": ("y1",), "up1": ("down0",),
+    "down1": ("down0",), "back1": ("back0",), "up_other": ("down_other", "up1"),
+    "down_mine": ("up_other",), "up_mine": ("down_mine", "down_far"), "up_near": ("da0", "up_mine"),
+    "mid0": ("m1_sent",), "last": ("mid0",), "m2": ("last",), "mid1": ("m2_sent",),
+    "attn_near": ("m2",), "m3": ("attn_other",), "in_back": ("m3_sent",), "attn_mine": ("gain_sum",),
+    "gains": ("attn_mine",), "part_give": ("gains",), "m4": ("q1_sent",), "q2": ("m4_sent",),
+    "tokens": ("q2_sent",), "q3": ("tokens",), "m_end": ("q3_sent",), "q4": ("m_end",),
+    "q1": ("m3_sent",), "attn_other": ("m1_sent",),
 }
 
 

time: 203 us -> 202 us (level)
  starting transfers between devices: 57.5 us -> 55.3 us
    ppermute x12, starting transfers between devices: 17.5 us -> 14 us  [step(): self.down = lax.ppermute(down, 'dp', ring.down)]
    ppermute x12, starting transfers between devices: 9.22 us -> 11.4 us  [step(): self.up = lax.ppermute(up, 'dp', ring.up)]
  transfers between devices with their start and end apart: 60 -> 60, of which waited for: 26 -> 29; matrix products, arithmetic and copies ran while one was open for 0% -> 0% of each run, Pallas kernels for 32% -> 32%
where the time goes in v1:
time: 202 us
  waiting for transfers between devices  73.7 us (36%)
  Pallas kernels  66.7 us (33%)
  starting transfers between devices  55.3 us (27%)
  local copies, waits for them, and re-layouts  5.18 us (3%)
    pallas_call x49, Pallas kernels, kernel_call(): pl.pallas_call(body, in_specs=[smem()] * smems + [whole()] * (len(args) -...  64.8 us
    ppermute x16, waiting for transfers between devices, step(): came.append(lax.ppermute(sent[way], 'dp', perm))  22.4 us
    ppermute x12, waiting for transfers between devices, step(): self.down = lax.ppermute(down, 'dp', ring.down)  20.6 us
    ppermute x9, waiting for transfers between devices, swap_sides(): return lax.ppermute(value, 'mp', [(0, 1), (1, 0)])  19.9 us
    ppermute x16, starting transfers between devices, step(): came.append(lax.ppermute(sent[way], 'dp', perm))  16 us
    ppermute x12, starting transfers between devices, step(): self.down = lax.ppermute(down, 'dp', ring.down)  14 us
    ppermute x9, starting transfers between devices, swap_sides(): return lax.ppermute(value, 'mp', [(0, 1), (1, 0)])  11.5 us
    ppermute x12, starting transfers between devices, step(): self.up = lax.ppermute(up, 'dp', ring.up)  11.4 us
  transfers between devices with their start and end apart: 60, of which 29 were waited for; matrix products, arithmetic and copies ran while one was open for 0% of the time, Pallas kernels for 32%

profile of v1, /device:TPU:0, one launch (start us, length us, event | category | flops | bytes accessed | tf_op | source)
XLA Modules:
  0.0 202.1 jit_solution(575595198457944801)
XLA Ops:
  2.7 3.0 %collective-permute-start.3 = (bf16[64,2048]{1,0:T(8,128)(2,1)S(1)}, bf16[64,2048]{1,0:T(8,128)(2,1)S(1)}, u32[]{:S(2)}, u32[]{:S(2)}) collective-permute-start(bf16[64,2048]{1,0:T(8,128)(2,1)S(1)} %stage.4.refs_0_), channel_id=1, source_target_pairs={{0,4},{2,6},{8,0},{10,2},{16,8},{18,10},{24,16},{26,18},{28,24},{3... | collective-permute-start | bytes 786440 | tf_op jit(solution)/shard_map/ppermute | solution.py:919
  7.9 4.2 %collective-permute-done.3.refs_2_ = bf16[64,2048]{1,0:T(8,128)(2,1)S(1)} collective-permute-done((bf16[64,2048]{1,0:T(8,128)(2,1)S(1)}, bf16[64,2048]{1,0:T(8,128)(2,1)S(1)}, u32[]{:S(2)}, u32[]{:S(2)}) %collective-permute-start.3) | collective-permute-done | bytes 262176 | tf_op jit(solution)/shard_map/ppermute | solution.py:919
  12.1 1.7 collective-permute-start.5
  14.1 1.7 collective-permute-start.4
  17.2 2.4 %prepare.1 = (bf16[512,1024]{1,0:T(8,128)(2,1)S(1)}, bf16[512,1024]{1,0:T(8,128)(2,1)S(1)}, f32[4,1024]{1,0:T(4,128)S(1)}, f32[4,1024]{1,0:T(4,128)S(1)}) custom-call(s32[2]{0:T(128)S(1)} %pad_add_fusion.ids_ref, bf16[512,1024]{1,0:T(8,128)(2,1)S(1)} %copy-done, f32[4,1024]{1,0:T(4,128)S(1)} %copy-done.6, f32[4,1024]{1,0:T(4,128)S(1)} %copy-done.7), custom_call_target="tpu_custom_call" | custom-call | bytes 12177000 | tf_op jit(solution)/shard_map/prepare/pallas_call | solution.py:77
  19.6 1.5 collective-permute-start.6
  21.7 4.4 %collective-permute-done.6.down_ref.refs_6_ = bf16[64,2048]{1,0:T(8,128)(2,1)S(1)} collective-permute-done((bf16[64,2048]{1,0:T(8,128)(2,1)S(1)}, bf16[64,2048]{1,0:T(8,128)(2,1)S(1)}, u32[]{:S(2)}, u32[]{:S(2)}) %collective-permute-start.6) | collective-permute-done | bytes 262176 | tf_op jit(solution)/shard_map/ppermute | solution.py:919
  29.8 1.7 collective-permute-start.10
  31.8 4.7 %collective-permute-done.10.refs_8_ = bf16[32,2048]{1,0:T(8,128)(2,1)S(1)} collective-permute-done((bf16[32,2048]{1,0:T(8,128)(2,1)S(1)}, bf16[32,2048]{1,0:T(8,128)(2,1)S(1)}, u32[]{:S(2)}, u32[]{:S(2)}) %collective-permute-start.10) | collective-permute-done | bytes 131104 | tf_op jit(solution)/shard_map/ppermute | solution.py:919
  37.3 1.6 collective-permute-start.14
  42.1 1.6 rotary.1
  44.3 2.0 qkv_project.1.q_ref
  46.3 2.5 %attend0.1 = (bf16[8,256,256]{2,1,0:T(8,128)(2,1)S(1)}, bf16[256,512]{1,0:T(8,128)(2,1)S(1)}, bf16[256,1024]{1,0:T(8,128)(2,1)S(1)}) custom-call(s32[4]{0:T(128)S(1)} %copy-done.8, bf16[512,1536]{1,0:T(8,128)(2,1)S(1)} %qkv_project.1.q_ref, bf16[512,2048]{1,0:T(8,128)(2,1)S(1)} %assemble.3.refs_0_, bf16[512,2048]{1,0:T(8,128)(2,1)S(1)} %collective-permute-done.13.refs_1_), custom_call_target="tpu_custom_call" | custom-call | bytes 9225000 | tf_op jit(solution)/shard_map/attend0/pallas_call | solution.py:77
  48.8 1.6 collective-permute-start.18
  50.4 1.6 collective-permute-start.22
  52.4 4.4 %attend1.1 = (bf16[8,256,512]{2,1,0:T(8,128)(2,1)S(1)}, bf16[256,512]{1,0:T(8,128)(2,1)S(1)}, bf16[256,1024]{1,0:T(8,128)(2,1)S(1)}) custom-call(s32[4]{0:T(128)S(1)} %copy-done.8, bf16[512,1536]{1,0:T(8,128)(2,1)S(1)} %qkv_project.1.q_ref, bf16[512,2048]{1,0:T(8,128)(2,1)S(1)} %assemble.3.refs_0_, bf16[512,2048]{1,0:T(8,128)(2,1)S(1)} %collective-permute-done.13.refs_1_), custom_call_target="tpu_custom_call" | custom-call | bytes 16236000 | tf_op jit(solution)/shard_map/attend1/pallas_call | solution.py:77
  59.9 1.7 collective-permute-start.24
  61.5 4.6 %collective-permute-done.17.down_ref.refs_6_ = bf16[64,2048]{1,0:T(8,128)(2,1)S(1)} collective-permute-done((bf16[64,2048]{1,0:T(8,128)(2,1)S(1)}, bf16[64,2048]{1,0:T(8,128)(2,1)S(1)}, u32[]{:S(2)}, u32[]{:S(2)}) %collective-permute-start.17) | collective-permute-done | bytes 262176 | tf_op jit(solution)/shard_map/ppermute | solution.py:919
  66.1 1.6 collective-permute-start.25
  67.7 1.6 collective-permute-start.19
  69.8 4.3 %collective-permute-done.19.refs_7_ = bf16[32,2048]{1,0:T(8,128)(2,1)S(1)} collective-permute-done((bf16[32,2048]{1,0:T(8,128)(2,1)S(1)}, bf16[32,2048]{1,0:T(8,128)(2,1)S(1)}, u32[]{:S(2)}, u32[]{:S(2)}) %collective-permute-start.19) | collective-permute-done | bytes 131104 | tf_op jit(solution)/shard_map/ppermute | solution.py:918
  75.0 1.5 collective-permute-start.27
  77.0 2.9 %collective-permute-done.27.refs_7_ = bf16[32,2048]{1,0:T(8,128)(2,1)S(1)} collective-permute-done((bf16[32,2048]{1,0:T(8,128)(2,1)S(1)}, bf16[32,2048]{1,0:T(8,128)(2,1)S(1)}, u32[]{:S(2)}, u32[]{:S(2)}) %collective-permute-start.27) | collective-permute-done | bytes 131104 | tf_op jit(solution)/shard_map/ppermute | solution.py:918
  83.1 2.6 %up_project.2 = (bf16[256,2048]{1,0:T(8,128)(2,1)S(1)}, bf16[256,2048]{1,0:T(8,128)(2,1)S(1)}) custom-call(bf16[256,1024]{1,0:T(8,128)(2,1)S(1)} %mid_norm.2.a3_ref.refs_0_, bf16[512,2048]{1,0:T(8,128)(2,1)S(1)} %assemble.4.refs_0_.refs_2_, bf16[512,2048]{1,0:T(8,128)(2,1)S(1)} %collective-permute-done.21.refs_1_.refs_3_), custom_call_target="tpu_custom_call" | custom-call | bytes 15867000 | tf_op jit(solution)/shard_map/up_project/pallas_call | solution.py:77
  89.6 2.6 %up_project.3 = (bf16[256,2048]{1,0:T(8,128)(2,1)S(1)}, bf16[256,2048]{1,0:T(8,128)(2,1)S(1)}) custom-call(bf16[256,1024]{1,0:T(8,128)(2,1)S(1)} %mid_norm.3.a3_ref.refs_1_, bf16[512,2048]{1,0:T(8,128)(2,1)S(1)} %assemble.4.refs_0_.refs_2_, bf16[512,2048]{1,0:T(8,128)(2,1)S(1)} %collective-permute-done.21.refs_1_.refs_3_), custom_call_target="tpu_custom_call" | custom-call | bytes 15867000 | tf_op jit(solution)/shard_map/up_project/pallas_call | solution.py:77
  94.6 7.8 %collective-permute-done.30.zb_ref.refs_5_ = bf16[256,1024]{1,0:T(8,128)(2,1)S(1)} collective-permute-done((bf16[256,1024]{1,0:T(8,128)(2,1)S(1)}, bf16[256,1024]{1,0:T(8,128)(2,1)S(1)}, u32[]{:S(2)}, u32[]{:S(2)}) %collective-permute-start.30) | collective-permute-done | bytes 524320 | tf_op jit(solution)/shard_map/ppermute | solution.py:972
  102.4 3.8 %mlp_back.2 = (bf16[256,1024]{1,0:T(8,128)(2,1)S(1)}, bf16[256,2048]{1,0:T(8,128)(2,1)S(1)}, bf16[256,1024]{1,0:T(8,128)(2,1)S(1)}) custom-call(bf16[256,1024]{1,0:T(8,128)(2,1)S(1)} %down_project.2.za_ref.refs_4_, bf16[256,1024]{1,0:T(8,128)(2,1)S(1)} %collective-permute-done.30.zb_ref.refs_5_, bf16[512,1024]{1,0:T(8,128)(2,1)S(1)} %cotangent_rows.1.cot_ref, ...), custom_call_target="tpu_custom_call" | custom-call | bytes 19926000 | tf_op jit(solution)/shard_map/mlp_back/pallas_call | solution.py:77
  107.2 6.4 %collective-permute-done.31.zb_ref.refs_7_ = bf16[256,1024]{1,0:T(8,128)(2,1)S(1)} collective-permute-done((bf16[256,1024]{1,0:T(8,128)(2,1)S(1)}, bf16[256,1024]{1,0:T(8,128)(2,1)S(1)}, u32[]{:S(2)}, u32[]{:S(2)}) %collective-permute-start.31) | collective-permute-done | bytes 524320 | tf_op jit(solution)/shard_map/ppermute | solution.py:972
  113.6 3.8 %mlp_back.3 = (bf16[256,1024]{1,0:T(8,128)(2,1)S(1)}, bf16[256,2048]{1,0:T(8,128)(2,1)S(1)}, bf16[256,1024]{1,0:T(8,128)(2,1)S(1)}) custom-call(bf16[256,1024]{1,0:T(8,128)(2,1)S(1)} %down_project.3.za_ref.refs_6_, bf16[256,1024]{1,0:T(8,128)(2,1)S(1)} %collective-permute-done.31.zb_ref.refs_7_, bf16[512,1024]{1,0:T(8,128)(2,1)S(1)} %cotangent_rows.1.cot_ref, ...), custom_call_target="tpu_custom_call" | custom-call | bytes 19926000 | tf_op jit(solution)/shard_map/mlp_back/pallas_call | solution.py:77
  117.4 1.6 weight_grad.6
  119.1 1.6 weight_grad.7
  121.3 1.6 weight_grad.8
  122.9 1.6 weight_grad.9
  126.8 1.9 collective-permute-start.37
  128.6 2.3 %mid_back.2 = (f32[256,1024]{1,0:T(8,128)S(1)}, bf16[256,1024]{1,0:T(8,128)(2,1)S(1)}, bf16[256,512]{1,0:T(8,128)(2,1)S(1)}, f32[4,8,1024]{2,1,0:T(8,128)S(1)}) custom-call(bf16[512,1024]{1,0:T(8,128)(2,1)S(1)} %get-tuple-element.196.x_ref, bf16[256,1024]{1,0:T(8,128)(2,1)S(1)} %get-tuple-element.142.ya_ref.refs_0_, ...), custom_call_target="tpu_custom_call" | custom-call | bytes 12177000 | tf_op jit(solution)/shard_map/mid_back/pallas_call | solution.py:77
  131.0 3.3 %last_norm.1 = (bf16[256,1024]{1,0:T(8,128)(2,1)}, f32[2,8,1024]{2,1,0:T(8,128)S(1)}) custom-call(s32[2]{0:T(128)S(1)} %pad_add_fusion.ids_ref, bf16[512,1024]{1,0:T(8,128)(2,1)S(1)} %get-tuple-element.196.x_ref, bf16[512,1024]{1,0:T(8,128)(2,1)S(1)} %cotangent_rows.1.cot_ref, f32[4,1024]{1,0:T(4,128)S(1)} %get-tuple-element.153.gain_ref, ...), custom_call_target="tpu_custom_call" | custom-call | bytes 11070000 | tf_op jit(solution)/shard_map/last_norm/pallas_call | solution.py:77
  135.1 1.6 collective-permute-start.40
  136.7 2.3 %collective-permute-done.39.eb_ref = bf16[256,1024]{1,0:T(8,128)(2,1)S(1)} collective-permute-done((bf16[256,1024]{1,0:T(8,128)(2,1)S(1)}, bf16[256,1024]{1,0:T(8,128)(2,1)S(1)}, u32[]{:S(2)}, u32[]{:S(2)}) %collective-permute-start.39) | collective-permute-done | bytes 524320 | tf_op jit(solution)/shard_map/ppermute | solution.py:972
  139.0 2.3 %mid_back.3 = (f32[256,1024]{1,0:T(8,128)S(1)}, bf16[256,1024]{1,0:T(8,128)(2,1)S(1)}, bf16[256,512]{1,0:T(8,128)(2,1)S(1)}, f32[4,8,1024]{2,1,0:T(8,128)S(1)}) custom-call(bf16[512,1024]{1,0:T(8,128)(2,1)S(1)} %get-tuple-element.196.x_ref, bf16[256,1024]{1,0:T(8,128)(2,1)S(1)} %get-tuple-element.156.ya_ref.refs_2_, ...), custom_call_target="tpu_custom_call" | custom-call | bytes 12177000 | tf_op jit(solution)/shard_map/mid_back/pallas_call | solution.py:77
  141.4 5.9 %attend_back.1.refs_1_.g_ref = bf16[512,1536]{1,0:T(8,128)(2,1)S(1)} custom-call(bf16[512,1536]{1,0:T(8,128)(2,1)S(1)} %qkv_project.1.q_ref, bf16[8,256,256]{2,1,0:T(8,128)(2,1)S(1)} %get-tuple-element.184.p0_ref, bf16[8,256,512]{2,1,0:T(8,128)(2,1)S(1)} %get-tuple-element.185.p1_ref, bf16[256,512]{1,0:T(8,128)(2,1)S(1)} %get-tuple-element.186.o0.refs_4_, ...), custom_call_target="tpu_custom_call" | custom-call | bytes 18450000 | tf_op jit(solution)/shard_map/attend_back/pallas_call | solution.py:77
  152.9 3.6 %in_back.1 = (bf16[256,1024]{1,0:T(8,128)(2,1)S(1)}, bf16[256,1024]{1,0:T(8,128)(2,1)S(1)}, f32[2,8,1024]{2,1,0:T(8,128)S(1)}) custom-call(s32[2]{0:T(128)S(1)} %pad_add_fusion.ids_ref, bf16[512,1536]{1,0:T(8,128)(2,1)S(1)} %attend_back.1.refs_1_.g_ref, bf16[512,1024]{1,0:T(8,128)(2,1)S(1)} %get-tuple-element.196.x_ref, ...), custom_call_target="tpu_custom_call" | custom-call | bytes 13284000 | tf_op jit(solution)/shard_map/in_back/pallas_call | solution.py:77
  162.8 1.9 collective-permute-done.47.refs_8_
  166.5 1.7 collective-permute-done.50.refs_5_
  171.3 1.7 collective-permute-start.52
  173.4 2.2 %collective-permute-done.51.got_ref = bf16[256,1024]{1,0:T(8,128)(2,1)S(1)} collective-permute-done((bf16[256,1024]{1,0:T(8,128)(2,1)S(1)}, bf16[256,1024]{1,0:T(8,128)(2,1)S(1)}, u32[]{:S(2)}, u32[]{:S(2)}) %collective-permute-start.51) | collective-permute-done | bytes 524320 | tf_op jit(solution)/shard_map/ppermute | solution.py:972
  175.5 2.8 %tokens_back.1 = f32[256,1024]{1,0:T(8,128)} custom-call(s32[2]{0:T(128)S(1)} %pad_add_fusion.ids_ref, bf16[512,1024]{1,0:T(8,128)(2,1)S(1)} %get-tuple-element.196.x_ref, bf16[256,1024]{1,0:T(8,128)(2,1)S(1)} %get-tuple-element.221.keep_ref, bf16[256,1024]{1,0:T(8,128)(2,1)S(1)} %collective-permute-done.51.got_ref, ...), custom_call_target="tpu_custom_call" | custom-call | bytes 14391000 | tf_op jit(solution)/shard_map/tokens_back/pallas_call | solution.py:77
  181.1 9.8 %collective-permute-done.52.refs_8_ = bf16[64,4096]{1,0:T(8,128)(2,1)S(1)} collective-permute-done((bf16[64,4096]{1,0:T(8,128)(2,1)S(1)}, bf16[64,4096]{1,0:T(8,128)(2,1)S(1)}, u32[]{:S(2)}, u32[]{:S(2)}) %collective-permute-start.52) | collective-permute-done | bytes 524320 | tf_op jit(solution)/shard_map/ppermute | solution.py:951
  195.9 4.6 %collective-permute-done.59.refs_6_ = bf16[64,2176]{1,0:T(8,128)(2,1)S(1)} collective-permute-done((bf16[64,2176]{1,0:T(8,128)(2,1)S(1)}, bf16[64,2176]{1,0:T(8,128)(2,1)S(1)}, u32[]{:S(2)}, u32[]{:S(2)}) %collective-permute-start.59) | collective-permute-done | bytes 278560 | tf_op jit(solution)/shard_map/ppermute | solution.py:951
  (146 shorter events, 60.7 us)
Async XLA Ops:
  2.7 9.4 %collective-permute-start.3 = (bf16[64,2048]{1,0:T(8,128)(2,1)S(1)}, bf16[64,2048]{1,0:T(8,128)(2,1)S(1)}, u32[]{:S(2)}, u32[]{:S(2)}) collective-permute-start(bf16[64,2048]{1,0:T(8,128)(2,1)S(1)} %stage.4.refs_0_), channel_id=1, source_target_pairs={{0,4},{2,6},{8,0},{10,2},{16,8},{18,10},{24,16},{26,18},{28,24},{3... | collective-permute-start | bytes 786440 | tf_op jit(solution)/shard_map/ppermute | solution.py:919
  5.7 8.0 %collective-permute-start = (bf16[64,2048]{1,0:T(8,128)(2,1)S(1)}, bf16[64,2048]{1,0:T(8,128)(2,1)S(1)}, u32[]{:S(2)}, u32[]{:S(2)}) collective-permute-start(bf16[64,2048]{1,0:T(8,128)(2,1)S(1)} %stage.4.refs_0_), channel_id=1, source_target_pairs={{0,8},{2,10},{8,16},{10,18},{16,24},{18,26},{24,28},{26,30},{28,20... | collective-permute-start | bytes 786440 | tf_op jit(solution)/shard_map/ppermute | solution.py:918
  12.1 7.6 %collective-permute-start.5 = (bf16[64,2048]{1,0:T(8,128)(2,1)S(1)}, bf16[64,2048]{1,0:T(8,128)(2,1)S(1)}, u32[]{:S(2)}, u32[]{:S(2)}) collective-permute-start(bf16[64,2048]{1,0:T(8,128)(2,1)S(1)} %collective-permute-done.3.refs_2_), channel_id=1, source_target_pairs={{0,4},{2,6},{8,0},{10,2},{16,8},{18,10},{24,16},{26,18},{28,24},{3... | collective-permute-start | bytes 786440 | tf_op jit(solution)/shard_map/ppermute | solution.py:919
  13.7 7.5 %collective-permute-start.1 = (bf16[64,2048]{1,0:T(8,128)(2,1)S(1)}, bf16[64,2048]{1,0:T(8,128)(2,1)S(1)}, u32[]{:S(2)}, u32[]{:S(2)}) collective-permute-start(bf16[64,2048]{1,0:T(8,128)(2,1)S(1)} %collective-permute-done.refs_1_), channel_id=1, source_target_pairs={{0,8},{2,10},{8,16},{10,18},{16,24},{18,26},{24,28},{26,30},{28,20... | collective-permute-start | bytes 786440 | tf_op jit(solution)/shard_map/ppermute | solution.py:918
  14.1 12.8 %collective-permute-start.4 = (bf16[256,1024]{1,0:T(8,128)(2,1)}, bf16[256,1024]{1,0:T(8,128)(2,1)S(1)}, u32[]{:S(2)}, u32[]{:S(2)}) collective-permute-start(bf16[256,1024]{1,0:T(8,128)(2,1)} %own_ref.1), channel_id=1, source_target_pairs={{0,1},{1,0},{2,3},{3,2},{4,5},{5,4},{6,7},{7,6},{8,9},{9,8},{10,11... | collective-permute-start | bytes 1572872 | tf_op jit(solution)/shard_map/ppermute | solution.py:972
  19.6 6.5 %collective-permute-start.6 = (bf16[64,2048]{1,0:T(8,128)(2,1)S(1)}, bf16[64,2048]{1,0:T(8,128)(2,1)S(1)}, u32[]{:S(2)}, u32[]{:S(2)}) collective-permute-start(bf16[64,2048]{1,0:T(8,128)(2,1)S(1)} %collective-permute-done.5.refs_4_), channel_id=1, source_target_pairs={{0,4},{2,6},{8,0},{10,2},{16,8},{18,10},{24,16},{26,18},{28,24},{3... | collective-permute-start | bytes 786440 | tf_op jit(solution)/shard_map/ppermute | solution.py:919
  21.2 6.5 %collective-permute-start.2 = (bf16[64,2048]{1,0:T(8,128)(2,1)S(1)}, bf16[64,2048]{1,0:T(8,128)(2,1)S(1)}, u32[]{:S(2)}, u32[]{:S(2)}) collective-permute-start(bf16[64,2048]{1,0:T(8,128)(2,1)S(1)} %collective-permute-done.1.refs_3_), channel_id=1, source_target_pairs={{0,8},{2,10},{8,16},{10,18},{16,24},{18,26},{24,28},{26,30},{28,20... | collective-permute-start | bytes 786440 | tf_op jit(solution)/shard_map/ppermute | solution.py:918
  27.7 9.4 %collective-permute-start.7 = (bf16[64,2048]{1,0:T(8,128)(2,1)S(1)}, bf16[64,2048]{1,0:T(8,128)(2,1)S(1)}, u32[]{:S(2)}, u32[]{:S(2)}) collective-permute-start(bf16[64,2048]{1,0:T(8,128)(2,1)S(1)} %stage.3.refs_0_), channel_id=1, source_target_pairs={{0,8},{2,10},{8,16},{10,18},{16,24},{18,26},{24,28},{26,30},{28,20... | collective-permute-start | bytes 786440 | tf_op jit(solution)/shard_map/ppermute | solution.py:918
  28.4 8.8 %collective-permute-start.8 = (bf16[64,2048]{1,0:T(8,128)(2,1)S(1)}, bf16[64,2048]{1,0:T(8,128)(2,1)S(1)}, u32[]{:S(2)}, u32[]{:S(2)}) collective-permute-start(bf16[64,2048]{1,0:T(8,128)(2,1)S(1)} %stage.3.refs_0_), channel_id=1, source_target_pairs={{0,4},{2,6},{8,0},{10,2},{16,8},{18,10},{24,16},{26,18},{28,24},{3... | collective-permute-start | bytes 786440 | tf_op jit(solution)/shard_map/ppermute | solution.py:919
  29.8 6.8 %collective-permute-start.10 = (bf16[32,2048]{1,0:T(8,128)(2,1)S(1)}, bf16[32,2048]{1,0:T(8,128)(2,1)S(1)}, u32[]{:S(2)}, u32[]{:S(2)}) collective-permute-start(bf16[32,2048]{1,0:T(8,128)(2,1)S(1)} %get-tuple-element.132), channel_id=1, source_target_pairs={{0,4},{2,6},{8,0},{10,2},{16,8},{18,10},{24,16},{26,18},{28,24},{3... | collective-permute-start | bytes 393224 | tf_op jit(solution)/shard_map/ppermute | solution.py:919
  37.2 7.1 %collective-permute-start.13 = (bf16[512,2048]{1,0:T(8,128)(2,1)S(1)}, bf16[512,2048]{1,0:T(8,128)(2,1)S(1)}, u32[]{:S(2)}, u32[]{:S(2)}) collective-permute-start(bf16[512,2048]{1,0:T(8,128)(2,1)S(1)} %assemble.3.refs_0_), channel_id=1, source_target_pairs={{0,2},{2,0},{4,6},{6,4},{8,10},{10,8},{12,14},{14,12},{16,18},{18,... | collective-permute-start | bytes 6291464 | tf_op jit(solution)/shard_map/ppermute | solution.py:896
  37.3 13.1 %collective-permute-start.14 = (bf16[64,2048]{1,0:T(8,128)(2,1)S(1)}, bf16[64,2048]{1,0:T(8,128)(2,1)S(1)}, u32[]{:S(2)}, u32[]{:S(2)}) collective-permute-start(bf16[64,2048]{1,0:T(8,128)(2,1)S(1)} %stage.5.refs_0_), channel_id=1, source_target_pairs={{0,8},{2,10},{8,16},{10,18},{16,24},{18,26},{24,28},{26,30},{28,20... | collective-permute-start | bytes 786440 | tf_op jit(solution)/shard_map/ppermute | solution.py:918
  38.9 13.1 %collective-permute-start.15 = (bf16[64,2048]{1,0:T(8,128)(2,1)S(1)}, bf16[64,2048]{1,0:T(8,128)(2,1)S(1)}, u32[]{:S(2)}, u32[]{:S(2)}) collective-permute-start(bf16[64,2048]{1,0:T(8,128)(2,1)S(1)} %stage.5.refs_0_), channel_id=1, source_target_pairs={{0,4},{2,6},{8,0},{10,2},{16,8},{18,10},{24,16},{26,18},{28,24},{3... | collective-permute-start | bytes 786440 | tf_op jit(solution)/shard_map/ppermute | solution.py:919
  39.3 17.5 %collective-permute-start.12 = (bf16[64,2048]{1,0:T(8,128)(2,1)S(1)}, bf16[64,2048]{1,0:T(8,128)(2,1)S(1)}, u32[]{:S(2)}, u32[]{:S(2)}) collective-permute-start(bf16[64,2048]{1,0:T(8,128)(2,1)S(1)} %collective-permute-done.8.refs_2_), channel_id=1, source_target_pairs={{0,4},{2,6},{8,0},{10,2},{16,8},{18,10},{24,16},{26,18},{28,24},{3... | collective-permute-start | bytes 786440 | tf_op jit(solution)/shard_map/ppermute | solution.py:919
  43.7 14.5 %collective-permute-start.11 = (bf16[64,2048]{1,0:T(8,128)(2,1)S(1)}, bf16[64,2048]{1,0:T(8,128)(2,1)S(1)}, u32[]{:S(2)}, u32[]{:S(2)}) collective-permute-start(bf16[64,2048]{1,0:T(8,128)(2,1)S(1)} %collective-permute-done.7.refs_1_), channel_id=1, source_target_pairs={{0,8},{2,10},{8,16},{10,18},{16,24},{18,26},{24,28},{26,30},{28,20... | collective-permute-start | bytes 786440 | tf_op jit(solution)/shard_map/ppermute | solution.py:918
  48.8 18.9 %collective-permute-start.18 = (bf16[256,1024]{1,0:T(8,128)(2,1)S(1)}, bf16[256,1024]{1,0:T(8,128)(2,1)S(1)}, u32[]{:S(2)}, u32[]{:S(2)}) collective-permute-start(bf16[256,1024]{1,0:T(8,128)(2,1)S(1)} %get-tuple-element.142.ya_ref.refs_0_), channel_id=1, source_target_pairs={{0,1},{1,0},{2,3},{3,2},{4,5},{5,4},{6,7},{7,6},{8,9},{9,8},{10,11... | collective-permute-start | bytes 1572872 | tf_op jit(solution)/shard_map/ppermute | solution.py:972
  50.4 8.5 %collective-permute-start.22 = (bf16[64,2048]{1,0:T(8,128)(2,1)S(1)}, bf16[64,2048]{1,0:T(8,128)(2,1)S(1)}, u32[]{:S(2)}, u32[]{:S(2)}) collective-permute-start(bf16[64,2048]{1,0:T(8,128)(2,1)S(1)} %collective-permute-done.14.refs_1_), channel_id=1, source_target_pairs={{0,8},{2,10},{8,16},{10,18},{16,24},{18,26},{24,28},{26,30},{28,20... | collective-permute-start | bytes 786440 | tf_op jit(solution)/shard_map/ppermute | solution.py:918
  52.0 7.9 %collective-permute-start.23 = (bf16[64,2048]{1,0:T(8,128)(2,1)S(1)}, bf16[64,2048]{1,0:T(8,128)(2,1)S(1)}, u32[]{:S(2)}, u32[]{:S(2)}) collective-permute-start(bf16[64,2048]{1,0:T(8,128)(2,1)S(1)} %collective-permute-done.15.refs_2_), channel_id=1, source_target_pairs={{0,4},{2,6},{8,0},{10,2},{16,8},{18,10},{24,16},{26,18},{28,24},{3... | collective-permute-start | bytes 786440 | tf_op jit(solution)/shard_map/ppermute | solution.py:919
  56.8 9.3 %collective-permute-start.17 = (bf16[64,2048]{1,0:T(8,128)(2,1)S(1)}, bf16[64,2048]{1,0:T(8,128)(2,1)S(1)}, u32[]{:S(2)}, u32[]{:S(2)}) collective-permute-start(bf16[64,2048]{1,0:T(8,128)(2,1)S(1)} %collective-permute-done.12.refs_4_), channel_id=1, source_target_pairs={{0,4},{2,6},{8,0},{10,2},{16,8},{18,10},{24,16},{26,18},{28,24},{3... | collective-permute-start | bytes 786440 | tf_op jit(solution)/shard_map/ppermute | solution.py:919
  58.1 9.6 %collective-permute-start.16 = (bf16[64,2048]{1,0:T(8,128)(2,1)S(1)}, bf16[64,2048]{1,0:T(8,128)(2,1)S(1)}, u32[]{:S(2)}, u32[]{:S(2)}) collective-permute-start(bf16[64,2048]{1,0:T(8,128)(2,1)S(1)} %collective-permute-done.11.refs_3_), channel_id=1, source_target_pairs={{0,8},{2,10},{8,16},{10,18},{16,24},{18,26},{24,28},{26,30},{28,20... | collective-permute-start | bytes 786440 | tf_op jit(solution)/shard_map/ppermute | solution.py:918
  59.9 17.2 %collective-permute-start.24 = (bf16[256,1024]{1,0:T(8,128)(2,1)S(1)}, bf16[256,1024]{1,0:T(8,128)(2,1)S(1)}, u32[]{:S(2)}, u32[]{:S(2)}) collective-permute-start(bf16[256,1024]{1,0:T(8,128)(2,1)S(1)} %get-tuple-element.156.ya_ref.refs_2_), channel_id=1, source_target_pairs={{0,1},{1,0},{2,3},{3,2},{4,5},{5,4},{6,7},{7,6},{8,9},{9,8},{10,11... | collective-permute-start | bytes 1572872 | tf_op jit(solution)/shard_map/ppermute | solution.py:972
  61.5 13.4 %collective-permute-start.26 = (bf16[64,2048]{1,0:T(8,128)(2,1)S(1)}, bf16[64,2048]{1,0:T(8,128)(2,1)S(1)}, u32[]{:S(2)}, u32[]{:S(2)}) collective-permute-start(bf16[64,2048]{1,0:T(8,128)(2,1)S(1)} %collective-permute-done.23.refs_4_), channel_id=1, source_target_pairs={{0,4},{2,6},{8,0},{10,2},{16,8},{18,10},{24,16},{26,18},{28,24},{3... | collective-permute-start | bytes 786440 | tf_op jit(solution)/shard_map/ppermute | solution.py:919
  66.1 8.8 %collective-permute-start.25 = (bf16[64,2048]{1,0:T(8,128)(2,1)S(1)}, bf16[64,2048]{1,0:T(8,128)(2,1)S(1)}, u32[]{:S(2)}, u32[]{:S(2)}) collective-permute-start(bf16[64,2048]{1,0:T(8,128)(2,1)S(1)} %collective-permute-done.22.refs_3_), channel_id=1, source_target_pairs={{0,8},{2,10},{8,16},{10,18},{16,24},{18,26},{24,28},{26,30},{28,20... | collective-permute-start | bytes 786440 | tf_op jit(solution)/shard_map/ppermute | solution.py:918
  67.7 6.4 %collective-permute-start.19 = (bf16[32,2048]{1,0:T(8,128)(2,1)S(1)}, bf16[32,2048]{1,0:T(8,128)(2,1)S(1)}, u32[]{:S(2)}, u32[]{:S(2)}) collective-permute-start(bf16[32,2048]{1,0:T(8,128)(2,1)S(1)} %get-tuple-element.150), channel_id=1, source_target_pairs={{0,8},{2,10},{8,16},{10,18},{16,24},{18,26},{24,28},{26,30},{28,20... | collective-permute-start | bytes 393224 | tf_op jit(solution)/shard_map/ppermute | solution.py:918
  77.0 6.0 %collective-permute-start.21 = (bf16[512,2048]{1,0:T(8,128)(2,1)S(1)}, bf16[512,2048]{1,0:T(8,128)(2,1)S(1)}, u32[]{:S(2)}, u32[]{:S(2)}) collective-permute-start(bf16[512,2048]{1,0:T(8,128)(2,1)S(1)} %assemble.4.refs_0_.refs_2_), channel_id=1, source_target_pairs={{0,2},{2,0},{4,6},{6,4},{8,10},{10,8},{12,14},{14,12},{16,18},{18,... | collective-permute-start | bytes 6291464 | tf_op jit(solution)/shard_map/ppermute | solution.py:896
  87.5 14.8 %collective-permute-start.30 = (bf16[256,1024]{1,0:T(8,128)(2,1)S(1)}, bf16[256,1024]{1,0:T(8,128)(2,1)S(1)}, u32[]{:S(2)}, u32[]{:S(2)}) collective-permute-start(bf16[256,1024]{1,0:T(8,128)(2,1)S(1)} %down_project.2.za_ref.refs_4_), channel_id=1, source_target_pairs={{0,1},{1,0},{2,3},{3,2},{4,5},{5,4},{6,7},{7,6},{8,9},{9,8},{10,11... | collective-permute-start | bytes 1572872 | tf_op jit(solution)/shard_map/ppermute | solution.py:972
  93.5 20.1 %collective-permute-start.31 = (bf16[256,1024]{1,0:T(8,128)(2,1)S(1)}, bf16[256,1024]{1,0:T(8,128)(2,1)S(1)}, u32[]{:S(2)}, u32[]{:S(2)}) collective-permute-start(bf16[256,1024]{1,0:T(8,128)(2,1)S(1)} %down_project.3.za_ref.refs_6_), channel_id=1, source_target_pairs={{0,1},{1,0},{2,3},{3,2},{4,5},{5,4},{6,7},{7,6},{8,9},{9,8},{10,11... | collective-permute-start | bytes 1572872 | tf_op jit(solution)/shard_map/ppermute | solution.py:972
  106.1 18.5 %collective-permute-start.34 = (bf16[256,1024]{1,0:T(8,128)(2,1)S(1)}, bf16[256,1024]{1,0:T(8,128)(2,1)S(1)}, u32[]{:S(2)}, u32[]{:S(2)}) collective-permute-start(bf16[256,1024]{1,0:T(8,128)(2,1)S(1)} %get-tuple-element.180.ea_ref), channel_id=1, source_target_pairs={{0,1},{1,0},{2,3},{3,2},{4,5},{5,4},{6,7},{7,6},{8,9},{9,8},{10,11... | collective-permute-start | bytes 1572872 | tf_op jit(solution)/shard_map/ppermute | solution.py:972
  124.5 9.8 %collective-permute-start.35 = (bf16[448,2048]{1,0:T(8,128)(2,1)S(1)}, bf16[448,2048]{1,0:T(8,128)(2,1)S(1)}, u32[]{:S(2)}, u32[]{:S(2)}) collective-permute-start(bf16[448,2048]{1,0:T(8,128)(2,1)S(1)} %get-tuple-element.192), channel_id=1, source_target_pairs={{0,2},{2,0},{4,6},{6,4},{8,10},{10,8},{12,14},{14,12},{16,18},{18,... | collective-permute-start | bytes 5505032 | tf_op jit(solution)/shard_map/ppermute | solution.py:896
  124.6 9.7 %collective-permute-start.36 = (bf16[448,2048]{1,0:T(8,128)(2,1)S(1)}, bf16[448,2048]{1,0:T(8,128)(2,1)S(1)}, u32[]{:S(2)}, u32[]{:S(2)}) collective-permute-start(bf16[448,2048]{1,0:T(8,128)(2,1)S(1)} %get-tuple-element.195), channel_id=1, source_target_pairs={{0,2},{2,0},{4,6},{6,4},{8,10},{10,8},{12,14},{14,12},{16,18},{18,... | collective-permute-start | bytes 5505032 | tf_op jit(solution)/shard_map/ppermute | solution.py:896
  125.1 13.9 %collective-permute-start.39 = (bf16[256,1024]{1,0:T(8,128)(2,1)S(1)}, bf16[256,1024]{1,0:T(8,128)(2,1)S(1)}, u32[]{:S(2)}, u32[]{:S(2)}) collective-permute-start(bf16[256,1024]{1,0:T(8,128)(2,1)S(1)} %get-tuple-element.197.ea_ref), channel_id=1, source_target_pairs={{0,1},{1,0},{2,3},{3,2},{4,5},{5,4},{6,7},{7,6},{8,9},{9,8},{10,11... | collective-permute-start | bytes 1572872 | tf_op jit(solution)/shard_map/ppermute | solution.py:972
  126.2 8.1 %collective-permute-start.38 = (bf16[32,4096]{1,0:T(8,128)(2,1)S(1)}, bf16[32,4096]{1,0:T(8,128)(2,1)S(1)}, u32[]{:S(2)}, u32[]{:S(2)}) collective-permute-start(bf16[32,4096]{1,0:T(8,128)(2,1)S(1)} %ring_sum.17), channel_id=1, source_target_pairs={{0,4},{2,6},{8,0},{10,2},{16,8},{18,10},{24,16},{26,18},{28,24},{3... | collective-permute-start | bytes 786440 | tf_op jit(solution)/shard_map/ppermute | solution.py:951
  126.8 8.2 %collective-permute-start.37 = (bf16[32,4096]{1,0:T(8,128)(2,1)S(1)}, bf16[32,4096]{1,0:T(8,128)(2,1)S(1)}, u32[]{:S(2)}, u32[]{:S(2)}) collective-permute-start(bf16[32,4096]{1,0:T(8,128)(2,1)S(1)} %ring_sum.16), channel_id=1, source_target_pairs={{0,8},{2,10},{8,16},{10,18},{16,24},{18,26},{24,28},{26,30},{28,20... | collective-permute-start | bytes 786440 | tf_op jit(solution)/shard_map/ppermute | solution.py:951
  134.4 15.8 %collective-permute-start.41 = (bf16[64,4096]{1,0:T(8,128)(2,1)S(1)}, bf16[64,4096]{1,0:T(8,128)(2,1)S(1)}, u32[]{:S(2)}, u32[]{:S(2)}) collective-permute-start(bf16[64,4096]{1,0:T(8,128)(2,1)S(1)} %ring_sum.19), channel_id=1, source_target_pairs={{0,4},{2,6},{8,0},{10,2},{16,8},{18,10},{24,16},{26,18},{28,24},{3... | collective-permute-start | bytes 1572872 | tf_op jit(solution)/shard_map/ppermute | solution.py:951
  135.1 15.1 %collective-permute-start.40 = (bf16[64,4096]{1,0:T(8,128)(2,1)S(1)}, bf16[64,4096]{1,0:T(8,128)(2,1)S(1)}, u32[]{:S(2)}, u32[]{:S(2)}) collective-permute-start(bf16[64,4096]{1,0:T(8,128)(2,1)S(1)} %ring_sum.18), channel_id=1, source_target_pairs={{0,8},{2,10},{8,16},{10,18},{16,24},{18,26},{24,28},{26,30},{28,20... | collective-permute-start | bytes 1572872 | tf_op jit(solution)/shard_map/ppermute | solution.py:951
  150.2 17.9 %collective-permute-start.48 = (bf16[448,2048]{1,0:T(8,128)(2,1)S(1)}, bf16[448,2048]{1,0:T(8,128)(2,1)S(1)}, u32[]{:S(2)}, u32[]{:S(2)}) collective-permute-start(bf16[448,2048]{1,0:T(8,128)(2,1)S(1)} %get-tuple-element.219), channel_id=1, source_target_pairs={{0,2},{2,0},{4,6},{6,4},{8,10},{10,8},{12,14},{14,12},{16,18},{18,... | collective-permute-start | bytes 5505032 | tf_op jit(solution)/shard_map/ppermute | solution.py:896
  150.5 14.3 %collective-permute-start.47 = (bf16[64,4096]{1,0:T(8,128)(2,1)S(1)}, bf16[64,4096]{1,0:T(8,128)(2,1)S(1)}, u32[]{:S(2)}, u32[]{:S(2)}) collective-permute-start(bf16[64,4096]{1,0:T(8,128)(2,1)S(1)} %ring_sum.21), channel_id=1, source_target_pairs={{0,4},{2,6},{8,0},{10,2},{16,8},{18,10},{24,16},{26,18},{28,24},{3... | collective-permute-start | bytes 1572872 | tf_op jit(solution)/shard_map/ppermute | solution.py:951
  151.3 14.9 %collective-permute-start.46 = (bf16[64,4096]{1,0:T(8,128)(2,1)S(1)}, bf16[64,4096]{1,0:T(8,128)(2,1)S(1)}, u32[]{:S(2)}, u32[]{:S(2)}) collective-permute-start(bf16[64,4096]{1,0:T(8,128)(2,1)S(1)} %ring_sum.20), channel_id=1, source_target_pairs={{0,8},{2,10},{8,16},{10,18},{16,24},{18,26},{24,28},{26,30},{28,20... | collective-permute-start | bytes 1572872 | tf_op jit(solution)/shard_map/ppermute | solution.py:951
  161.2 14.4 %collective-permute-start.51 = (bf16[256,1024]{1,0:T(8,128)(2,1)S(1)}, bf16[256,1024]{1,0:T(8,128)(2,1)S(1)}, u32[]{:S(2)}, u32[]{:S(2)}) collective-permute-start(bf16[256,1024]{1,0:T(8,128)(2,1)S(1)} %get-tuple-element.223), channel_id=1, source_target_pairs={{0,1},{1,0},{2,3},{3,2},{4,5},{5,4},{6,7},{7,6},{8,9},{9,8},{10,11... | collective-permute-start | bytes 1572872 | tf_op jit(solution)/shard_map/ppermute | solution.py:972
  162.3 5.8 %collective-permute-start.50 = (bf16[32,2176]{1,0:T(8,128)(2,1)S(1)}, bf16[32,2176]{1,0:T(8,128)(2,1)S(1)}, u32[]{:S(2)}, u32[]{:S(2)}) collective-permute-start(bf16[32,2176]{1,0:T(8,128)(2,1)S(1)} %ring_sum.23), channel_id=1, source_target_pairs={{0,4},{2,6},{8,0},{10,2},{16,8},{18,10},{24,16},{26,18},{28,24},{3... | collective-permute-start | bytes 417800 | tf_op jit(solution)/shard_map/ppermute | solution.py:951
  168.2 10.1 %collective-permute-start.54 = (bf16[64,2176]{1,0:T(8,128)(2,1)S(1)}, bf16[64,2176]{1,0:T(8,128)(2,1)S(1)}, u32[]{:S(2)}, u32[]{:S(2)}) collective-permute-start(bf16[64,2176]{1,0:T(8,128)(2,1)S(1)} %ring_sum.27), channel_id=1, source_target_pairs={{0,4},{2,6},{8,0},{10,2},{16,8},{18,10},{24,16},{26,18},{28,24},{3... | collective-permute-start | bytes 835592 | tf_op jit(solution)/shard_map/ppermute | solution.py:951
  170.0 9.6 %collective-permute-start.53 = (bf16[64,2176]{1,0:T(8,128)(2,1)S(1)}, bf16[64,2176]{1,0:T(8,128)(2,1)S(1)}, u32[]{:S(2)}, u32[]{:S(2)}) collective-permute-start(bf16[64,2176]{1,0:T(8,128)(2,1)S(1)} %ring_sum.26), channel_id=1, source_target_pairs={{0,8},{2,10},{8,16},{10,18},{16,24},{18,26},{24,28},{26,30},{28,20... | collective-permute-start | bytes 835592 | tf_op jit(solution)/shard_map/ppermute | solution.py:951
  171.3 19.6 %collective-permute-start.52 = (bf16[64,4096]{1,0:T(8,128)(2,1)S(1)}, bf16[64,4096]{1,0:T(8,128)(2,1)S(1)}, u32[]{:S(2)}, u32[]{:S(2)}) collective-permute-start(bf16[64,4096]{1,0:T(8,128)(2,1)S(1)} %ring_sum.24), channel_id=1, source_target_pairs={{0,8},{2,10},{8,16},{10,18},{16,24},{18,26},{24,28},{26,30},{28,20... | collective-permute-start | bytes 1572872 | tf_op jit(solution)/shard_map/ppermute | solution.py:951
  173.0 17.9 %collective-permute-start.55 = (bf16[64,4096]{1,0:T(8,128)(2,1)S(1)}, bf16[64,4096]{1,0:T(8,128)(2,1)S(1)}, u32[]{:S(2)}, u32[]{:S(2)}) collective-permute-start(bf16[64,4096]{1,0:T(8,128)(2,1)S(1)} %ring_sum.25), channel_id=1, source_target_pairs={{0,4},{2,6},{8,0},{10,2},{16,8},{18,10},{24,16},{26,18},{28,24},{3... | collective-permute-start | bytes 1572872 | tf_op jit(solution)/shard_map/ppermute | solution.py:951
  178.4 14.9 %collective-permute-start.58 = (bf16[64,2176]{1,0:T(8,128)(2,1)S(1)}, bf16[64,2176]{1,0:T(8,128)(2,1)S(1)}, u32[]{:S(2)}, u32[]{:S(2)}) collective-permute-start(bf16[64,2176]{1,0:T(8,128)(2,1)S(1)} %ring_sum.29), channel_id=1, source_target_pairs={{0,4},{2,6},{8,0},{10,2},{16,8},{18,10},{24,16},{26,18},{28,24},{3... | collective-permute-start | bytes 835592 | tf_op jit(solution)/shard_map/ppermute | solution.py:951
  179.8 14.7 %collective-permute-start.56 = (bf16[64,2176]{1,0:T(8,128)(2,1)S(1)}, bf16[64,2176]{1,0:T(8,128)(2,1)S(1)}, u32[]{:S(2)}, u32[]{:S(2)}) collective-permute-start(bf16[64,2176]{1,0:T(8,128)(2,1)S(1)} %ring_sum.28), channel_id=1, source_target_pairs={{0,8},{2,10},{8,16},{10,18},{16,24},{18,26},{24,28},{26,30},{28,20... | collective-permute-start | bytes 835592 | tf_op jit(solution)/shard_map/ppermute | solution.py:951
  193.5 7.0 %collective-permute-start.59 = (bf16[64,2176]{1,0:T(8,128)(2,1)S(1)}, bf16[64,2176]{1,0:T(8,128)(2,1)S(1)}, u32[]{:S(2)}, u32[]{:S(2)}) collective-permute-start(bf16[64,2176]{1,0:T(8,128)(2,1)S(1)} %ring_sum.31), channel_id=1, source_target_pairs={{0,4},{2,6},{8,0},{10,2},{16,8},{18,10},{24,16},{26,18},{28,24},{3... | collective-permute-start | bytes 835592 | tf_op jit(solution)/shard_map/ppermute | solution.py:951
  194.6 6.6 %collective-permute-start.57 = (bf16[64,2176]{1,0:T(8,128)(2,1)S(1)}, bf16[64,2176]{1,0:T(8,128)(2,1)S(1)}, u32[]{:S(2)}, u32[]{:S(2)}) collective-permute-start(bf16[64,2176]{1,0:T(8,128)(2,1)S(1)} %ring_sum.30), channel_id=1, source_target_pairs={{0,8},{2,10},{8,16},{10,18},{16,24},{18,26},{24,28},{26,30},{28,20... | collective-permute-start | bytes 835592 | tf_op jit(solution)/shard_map/ppermute | solution.py:951
  (21 other events, 85.4 us)
